TPU v7x, 256 devices: a whole 4x4x8 slice. The times are simulated.
256 devices in a mesh: blk: 32 (over x_lo, z, core), uly: 8 (over y, x_hi).
Axes of the slice: x: 4 (x_hi: 2, x_lo: 2; x = x_hi * 2 + x_lo), y: 4, z: 8, core: 2. Of those that a mesh axis runs over, the one named last changes fastest.
Arguments:
- joint_qkv: bfloat16 [16384, 3, 3072], P(('blk', 'uly')), may hold values from -40 to 40
- text_count: int32 [1], replicated, may hold values from 1 to 512
- region_ids: int32 [16384], P('blk'), may hold values from 0 to 4
- region_identity: int32 [4], replicated, may hold values from 0 to 3, each once
- id_feats: bfloat16 [4, 256, 3072], P(None, 'blk'), may hold values from -6 to 6
- resample_mix: bfloat16 [32, 256], P(None, 'blk'), may hold values from -0.375 to 0.375
- latents: bfloat16 [32, 3072], replicated, may hold values from -6 to 6
- id_gain: float32 [3072], replicated, may hold values from 0.25 to 1.75
- id_kv_weight: bfloat16 [3072, 2, 3072], P(None, None, 'uly'), may hold values from -0.109375 to 0.109375
- out_weight: bfloat16 [3072, 3072], P('uly'), may hold values from -0.109375 to 0.109375
Outputs:
- output: bfloat16 [16384, 3072], P(('blk', 'uly'))
Inputs may be any that keep to these rules, and one draw needn't show every extreme that they name: `region_identity`: A permutation of 0 to 3.
All inputs are finite; a program needn't handle non-finite values.
Results may differ from a plain program's by a relative error of at most 0.0095.
Values may be sent and summed in bfloat16 or wider, within the bound.
No kernel may reach another device: no remote copies, remote signals or barrier semaphores. Data moves between devices by JAX's collectives and lax.ppermute only.
A program may use at most 128 MiB of HBM per device.

v0:
```python
import functools
import math

import jax
import jax.numpy as jnp
from jax import lax
from jax.experimental import pallas as pl
from jax.experimental.pallas import tpu as pltpu
from jax.sharding import Mesh
from jax.sharding import PartitionSpec as P

HEAD = 128
TXT = 512
SUBJ = 4
IDTOK = 32
SCALE2 = math.log2(math.e) / math.sqrt(HEAD)
SUB = 256
bf16 = jnp.bfloat16
f32 = jnp.float32
TRANSPOSED = (((1,), (1,)), ((), ()))
BLK = ("xl", "z", "c")
ULY = ("y", "xh")
SWAP = [(0, 1), (1, 0)]


def usable(count, mark):
    z, offset, size = mark
    text = (lax.axis_index("xl") == 0) & (lax.axis_index("c") == 0) & (lax.axis_index("z") == z)
    return jnp.where(text, jnp.clip(count - offset, 0, size), size)


def attn_kernel(pieces, marks, marks_all, first, last, sub, *refs):
    refs = list(refs)
    count = len(marks)
    text_count = refs.pop(0)
    q_refs = [refs.pop(0) for _ in range(pieces)]
    k_refs = [refs.pop(0) for _ in range(count)]
    v_refs = [refs.pop(0) for _ in range(count)]
    acc_in = None if first else refs.pop(0)
    if last:
        *shards, keep_ref, send_ref, lr_keep, lr_send, ones, acc_ref, k_buf, v_buf, top_ref = refs
    else:
        acc_ref, ones = refs
    head = pl.program_id(0)
    piece_rows = q_refs[0].shape[0]
    rows_here = pieces * piece_rows
    keys = [r.shape[0] for r in k_refs]

    @pl.when(head == 0)
    def _():
        at = 0
        for i in range(count):
            rows = lax.broadcasted_iota(jnp.int32, (keys[i], HEAD), 0)
            ones[at : at + keys[i], :] = jnp.where(rows < usable(text_count[0], marks[i]), 1.0, 0.0).astype(bf16)
            at += keys[i]

    def split(start):
        at = start % piece_rows
        q = q_refs[start // piece_rows][at : at + sub, :].astype(f32) * SCALE2
        high = q.astype(bf16)
        return jnp.concatenate([high, (q - high.astype(f32)).astype(bf16)], axis=1)

    def score(q, k):
        return lax.dot_general(q, jnp.concatenate([k, k], axis=1), TRANSPOSED, preferred_element_type=f32)

    for start in range(0, rows_here, sub):
        total = None if first else acc_in[start : start + sub, :]
        q = split(start)
        at = 0
        for i in range(count):
            p = jnp.exp2(score(q, k_refs[i][...])).astype(bf16)
            v = jnp.concatenate([v_refs[i][...], ones[at : at + keys[i], :]], axis=1)
            part = jnp.dot(p, v, preferred_element_type=f32)
            total = part if total is None else total + part
            at += keys[i]
        acc_ref[start : start + sub, :] = total

    if last:
        half = rows_here // 2

        def write(totals, references):
            keep_ref[...] = acc_ref[:half, 0:HEAD].astype(bf16)
            send_ref[...] = acc_ref[half:, 0:HEAD].astype(bf16)
            for ref, part in ((lr_keep, slice(0, half)), (lr_send, slice(half, 2 * half))):
                ref[0:1, :] = totals[:, part]
                ref[1:2, :] = references[:, part]

        totals = acc_ref[:, HEAD : 2 * HEAD].T[0:1, :]
        write(totals, jnp.zeros_like(totals))
        good = jnp.min(jnp.where((totals >= 2.0**-60) & (totals <= 2.0**100), 1.0, 0.0)) > 0.5

        @pl.when(jnp.logical_not(good))
        def _():
            acc_ref[...] = jnp.zeros_like(acc_ref)
            top_ref[...] = jnp.full_like(top_ref, -1e30)
            for i, shard in enumerate(shards):
                here = slice(0, shard.shape[0])
                key_at = pl.multiple_of(head * HEAD, HEAD)
                value_at = pl.multiple_of(shard.shape[1] // 2 + head * HEAD, HEAD)
                pltpu.sync_copy(shard.at[:, pl.ds(key_at, HEAD)], k_buf.at[here, :])
                pltpu.sync_copy(shard.at[:, pl.ds(value_at, HEAD)], v_buf.at[here, :])
                for start in range(0, rows_here, sub):
                    part = slice(start, start + sub)
                    scores = score(split(start), k_buf[here, :])
                    key = lax.broadcasted_iota(jnp.int32, scores.shape, 1)
                    scores = jnp.where(key < usable(text_count[0], marks_all[i]), scores, -1e30)
                    old = top_ref[part, 0:1]
                    new = jnp.maximum(old, jnp.max(scores, axis=1, keepdims=True))
                    p = jnp.exp2(scores - new).astype(bf16)
                    v = v_buf[here, :]
                    v = jnp.concatenate([v, jnp.ones_like(v)], axis=1)
                    added = jnp.dot(p, v, preferred_element_type=f32)
                    acc_ref[part, :] = acc_ref[part, :] * jnp.exp2(old - new) + added
                    top_ref[part, :] = jnp.broadcast_to(new, (sub, HEAD))
            write(acc_ref[:, HEAD : 2 * HEAD].T[0:1, :], top_ref[...].T[0:1, :])


def attend(text_count, queries, shards, acc, everything=None, sub=SUB):
    shards, marks = [kv for kv, _ in shards], [mark for _, mark in shards]
    first, last = acc is None, everything is not None
    marks_all = None
    pieces = len(queries)
    rows = pieces * queries[0].shape[0]
    heads = queries[0].shape[1] // HEAD
    acc_block = pl.BlockSpec((None, rows, 2 * HEAD), lambda h: (h, 0, 0))
    in_specs = [pl.BlockSpec(memory_space=pltpu.SMEM)]
    in_specs += [pl.BlockSpec((q.shape[0], HEAD), lambda h: (0, h)) for q in queries]
    args = [text_count] + list(queries)
    for shift in (0, heads):
        for kv in shards:
            in_specs.append(pl.BlockSpec((kv.shape[0], HEAD), lambda h, s=shift: (0, s + h)))
            args.append(kv)
    if not first:
        in_specs.append(acc_block)
        args.append(acc)
    total = sum(kv.shape[0] for kv in shards)
    scratch = [pltpu.VMEM((total, HEAD), bf16)]
    if last:
        in_specs += [pl.BlockSpec(memory_space=pl.ANY)] * len(everything)
        args += [kv for kv, _ in everything]
        marks_all = [mark for _, mark in everything]
        half = rows // 2
        out_specs = [pl.BlockSpec((half, HEAD), lambda h: (0, h))] * 2
        out_specs += [pl.BlockSpec((None, 2, half), lambda h: (h, 0, 0))] * 2
        out_shape = [jax.ShapeDtypeStruct((half, heads * HEAD), bf16)] * 2
        out_shape += [jax.ShapeDtypeStruct((heads, 2, half), f32)] * 2
        keys = everything[0][0].shape[0]
        scratch += [
            pltpu.VMEM((rows, 2 * HEAD), f32),
            pltpu.VMEM((keys, HEAD), bf16),
            pltpu.VMEM((keys, HEAD), bf16),
            pltpu.VMEM((rows, HEAD), f32),
        ]
    else:
        out_specs = acc_block
        out_shape = jax.ShapeDtypeStruct((heads, rows, 2 * HEAD), f32)
    return pl.pallas_call(
        functools.partial(attn_kernel, pieces, marks, marks_all, first, last, sub),
        grid=(heads,),
        in_specs=in_specs,
        out_specs=out_specs,
        out_shape=out_shape,
        scratch_shapes=scratch,
        cost_estimate=pl.CostEstimate(
            flops=heads * rows * total * (1 if first else 2048),
            bytes_accessed=(1 if first else 12) * 2**20,
            transcendentals=0 if first else heads * rows * total,
        ),
        compiler_params=pltpu.CompilerParams(vmem_limit_bytes=60 * 2**20),
    )(*args)


def id_kernel(q_ref, kv_ref, match_ref, out_ref):
    width = q_ref.shape[1]
    match = match_ref[...]
    lacking = 1.0 - jnp.max(match, axis=1, keepdims=True)
    for h in range(width // HEAD):
        cols = slice(h * HEAD, (h + 1) * HEAD)
        scores = lax.dot_general(
            q_ref[:, cols], kv_ref[:, cols], TRANSPOSED, preferred_element_type=f32
        ) * (1.0 / math.sqrt(HEAD))
        scores = jnp.where(match > 0, scores, -1e30)
        peak = jnp.max(scores, axis=1, keepdims=True)
        expo = jnp.exp(scores - peak) * match
        totals = jnp.sum(expo, axis=1, keepdims=True) + lacking
        v = kv_ref[:, width + h * HEAD : width + (h + 1) * HEAD]
        out_ref[:, cols] = jnp.dot(expo.astype(bf16), v, preferred_element_type=f32) / totals


def id_attend(q, id_kv, match):
    return pl.pallas_call(
        id_kernel,
        out_shape=jax.ShapeDtypeStruct(q.shape, f32),
        compiler_params=pltpu.CompilerParams(vmem_limit_bytes=32 * 2**20),
    )(q, id_kv, match)


def combine_kernel(keep, recv, lr_own, lr_core, lr_x, lr_far, id_ref, out_ref):
    slot = pl.program_id(0)
    tokens, width = keep.shape
    place = lax.rem(lax.axis_index("xl") + slot, 2)
    for h in range(width // HEAD):
        refs = [r[h, 1:2, :] for r in (lr_own, lr_core, lr_x, lr_far)]
        sums = [r[h, 0:1, :] for r in (lr_own, lr_core, lr_x, lr_far)]
        top = functools.reduce(jnp.maximum, refs)
        weight = [jnp.exp2(r - top) for r in refs]
        total = sum(w * s for w, s in zip(weight, sums))

        def column(row):
            return jnp.broadcast_to(row, (HEAD, tokens)).T

        cols = slice(h * HEAD, (h + 1) * HEAD)
        value = keep[:, cols].astype(f32) * column(weight[0] / total)
        value = value + recv[:, cols].astype(f32) * column(weight[1] / total)
        value = value + jnp.where(slot == 0, id_ref[:, cols], 0.0)
        out_ref[place, :, cols] = value.astype(bf16)


def combine(keep, recv, lr_keep, lr_core, lr_x, lr_far, idpart):
    tokens, width = idpart.shape
    heads = width // HEAD
    data = pl.BlockSpec((tokens, width), lambda s: (s, 0))
    near = pl.BlockSpec((heads, 2, tokens), lambda s: (0, 0, s))
    cross = pl.BlockSpec((heads, 2, tokens), lambda s: (0, 0, 1 - s))
    return pl.pallas_call(
        combine_kernel,
        grid=(2,),
        in_specs=[data, data, near, near, cross, cross, pl.BlockSpec((tokens, width), lambda s: (0, 0))],
        out_specs=pl.BlockSpec((2, tokens, width), lambda s: (0, 0, 0)),
        out_shape=jax.ShapeDtypeStruct((2, tokens, width), bf16),
        compiler_params=pltpu.CompilerParams(vmem_limit_bytes=60 * 2**20),
    )(keep, recv, lr_keep, lr_core, lr_x, lr_far, idpart)


def normalize(summed, id_gain):
    mean_square = jnp.mean(summed * summed, axis=-1, keepdims=True)
    return (summed * lax.rsqrt(mean_square + 1e-06) * id_gain).astype(bf16)


def pooled_terms(gathered, width):
    return lax.dot_general(
        gathered[:, width:], gathered[:, :width], (((0,), (0,)), ((), ())), preferred_element_type=f32
    )


def identity_rows(pooled, latents, id_gain, id_kv_weight):
    tokens = normalize(latents.astype(f32) + pooled, id_gain)
    return jnp.dot(tokens, id_kv_weight, preferred_element_type=f32).astype(bf16)


def project_kernel(mixed, weight, mine, other, product):
    xh = lax.axis_index("xh")
    groups = weight.shape[0]
    total = None
    for y in range(groups):
        group = (mixed[y].astype(f32) + mixed[groups + y].astype(f32)).astype(bf16)
        part = jnp.dot(group, weight[y], preferred_element_type=f32)
        total = part if total is None else total + part
    product[...] = total
    rows = mine.shape[0]
    mine[...] = product[pl.ds(pl.multiple_of(xh * rows, rows), rows), :]
    other[...] = product[pl.ds(pl.multiple_of((1 - xh) * rows, rows), rows), :].astype(bf16)


def project(mixed, weight, part, parts):
    tokens, width = mixed.shape[1] // 2, weight.shape[2] // parts
    tile = 512
    start = part * width // tile
    columns = pl.BlockSpec(weight.shape[:2] + (tile,), lambda n: (0, 0, start + n))
    out = pl.BlockSpec((tokens, tile), lambda n: (0, n))
    return pl.pallas_call(
        project_kernel,
        grid=(width // tile,),
        in_specs=[pl.BlockSpec(mixed.shape, lambda n: (0, 0, 0)), columns],
        out_specs=[out, out],
        out_shape=[
            jax.ShapeDtypeStruct((tokens, width), f32),
            jax.ShapeDtypeStruct((tokens, width), bf16),
        ],
        scratch_shapes=[pltpu.VMEM((2 * tokens, tile), f32)],
        cost_estimate=pl.CostEstimate(flops=2 * 10**9, bytes_accessed=10 * 2**20, transcendentals=0),
        compiler_params=pltpu.CompilerParams(vmem_limit_bytes=16 * 2**20),
    )(mixed, weight)


def on_device(
    joint_qkv,
    text_count,
    region_ids,
    region_identity,
    id_feats,
    resample_mix,
    latents,
    id_gain,
    id_kv_weight,
    out_weight,
):
    z_size = lax.axis_size("z")
    y_size = lax.axis_size("y")
    uly = y_size * lax.axis_size("xh")
    tok_dev = joint_qkv.shape[0]
    tok_blk = tok_dev * uly
    width = joint_qkv.shape[2]
    here = width // uly
    my_xl, my_z, my_c = lax.axis_index("xl"), lax.axis_index("z"), lax.axis_index("c")
    number = lax.axis_index(ULY)

    block = (my_xl * z_size + my_z) * 2 + my_c
    lanes = jnp.arange(SUBJ * IDTOK, dtype=jnp.int32) // IDTOK
    own_lanes = lanes[None, None, :] == jnp.arange(SUBJ, dtype=jnp.int32)[:, None, None]
    mix_rows = jnp.where(own_lanes, jnp.tile(resample_mix.T, (1, SUBJ))[None], 0)
    packed = jnp.concatenate([id_feats, mix_rows], axis=2)
    gathered = lax.all_gather(packed, "z", axis=0).reshape(-1, width + SUBJ * IDTOK)

    by_group = joint_qkv.reshape(tok_dev, 3, uly, here)
    position = block * tok_blk + number * tok_dev + jnp.arange(tok_dev, dtype=jnp.int32)
    used = (position >= TXT) | (position < text_count[0])
    values = jnp.where(used[:, None, None], by_group[:, 2], 0)
    sent = jnp.concatenate([by_group[:, 0], by_group[:, 1], values], axis=-1).transpose(1, 0, 2)
    got = lax.all_to_all(sent, ULY, 0, 0, tiled=True).reshape(tok_blk, 3 * here)

    position = block * tok_blk + jnp.arange(tok_blk, dtype=jnp.int32)
    has_id = (region_ids > 0) & (position >= TXT)
    subject = jnp.zeros((tok_blk,), jnp.int32)
    for which in range(SUBJ):
        subject = subject + jnp.where(region_ids == which + 1, region_identity[which], 0)
    key_subject = jnp.arange(SUBJ * IDTOK, dtype=jnp.int32) // IDTOK
    match = ((key_subject[None, :] == subject[:, None]) & has_id[:, None]).astype(f32)
    flat_weight = id_kv_weight.reshape(width, 2 * here)
    got, match, flat_weight, out_weight = lax.optimization_barrier((got, match, flat_weight, out_weight))
    weight = lax.all_gather(out_weight, "y", axis=0)
    q_own, kv = lax.optimization_barrier((got[:, :here], got[:, here:]))
    q_x = lax.ppermute(q_own, "xl", SWAP)
    queries = [q_own, q_x, lax.ppermute(q_own, "c", SWAP), lax.ppermute(q_x, "c", SWAP)]

    right = [(i, (i + 1) % z_size) for i in range(z_size)]
    left = [(i, (i - 1) % z_size) for i in range(z_size)]
    half = tok_blk // 2
    end = z_size // 2
    first = (kv, (0, 0, tok_blk))
    up, down, acc = kv, kv, None
    pending = [first]
    whole = []
    for step in range(1, end + 1):
        if step < end:
            up, down = lax.ppermute(up, "z", right), lax.ppermute(down, "z", left)
            arriving = [(up, (step, 0, tok_blk)), (down, (z_size - step, 0, tok_blk))]
        else:
            up, down = lax.ppermute(up[:half], "z", right), lax.ppermute(down[half:], "z", left)
            arriving = [(up, (end, 0, half)), (down, (end, half, half))]
        acc = attend(text_count, queries, pending, acc)
        if step == 1:
            up, down, acc, gathered = lax.optimization_barrier((up, down, acc, gathered))
        elif step < end:
            up, down, acc = lax.optimization_barrier((up, down, acc))
        if step < end:
            arriving = [(up, arriving[0][1]), (down, arriving[1][1])]
        whole += pending
        pending = arriving
    whole += pending
    terms = pooled_terms(gathered, width).reshape(2, 2, IDTOK, width)
    terms = jnp.where(my_c == 0, terms[:, 0], terms[:, 1]) + lax.ppermute(
        jnp.where(my_c == 0, terms[:, 1], terms[:, 0]), "c", SWAP
    )
    pooled = jnp.where(my_xl == 0, terms[0], terms[1]) + lax.ppermute(
        jnp.where(my_xl == 0, terms[1], terms[0]), "xl", SWAP
    )
    id_rows = identity_rows(pooled, latents, id_gain, flat_weight)
    id_core = lax.ppermute(id_rows, "c", SWAP)
    id_pair = jnp.where(my_c == 0, jnp.stack([id_rows, id_core]), jnp.stack([id_core, id_rows]))
    id_x = lax.ppermute(id_pair, "xl", SWAP)
    id_kv = jnp.where(my_xl == 0, jnp.stack([id_pair, id_x]), jnp.stack([id_x, id_pair]))
    id_kv = id_kv.reshape(SUBJ * IDTOK, 2 * here)
    idpart = id_attend(q_own, id_kv, match)

    idpart, acc = lax.optimization_barrier((idpart, acc))
    keep, send, lr_keep, lr_send = attend(text_count, queries, pending, acc, everything=whole)

    recv = lax.ppermute(send, "c", SWAP)
    lr_core = lax.ppermute(lr_send, "c", SWAP)
    lr_x = lax.ppermute(lr_keep, "xl", SWAP)
    lr_far = lax.ppermute(lr_send, ("xl", "c"), [(i, 3 - i) for i in range(4)])
    mixed = combine(keep, recv, lr_keep, lr_core, lr_x, lr_far, idpart)

    quarter = tok_blk // y_size
    mixed = mixed.reshape(2 * y_size, quarter, here)
    mixed = lax.all_to_all(mixed, ("xl", "y"), 0, 0, tiled=True)
    out = []
    for part in range(2):
        mine, other = project(mixed, weight, part, 2)
        out.append((mine + lax.ppermute(other, "xh", SWAP).astype(f32)).astype(bf16))
    return jnp.concatenate(out, axis=1)


def solution(mesh):
    fine = Mesh(mesh.devices.reshape(2, 8, 2, 4, 2), BLK + ULY)
    placed = (
        P(BLK + ULY, None, None),
        P(),
        P(BLK),
        P(),
        P(None, BLK, None),
        P(None, BLK),
        P(),
        P(),
        P(None, None, ULY),
        P(ULY, None),
    )
    return jax.shard_map(
        on_device, mesh=fine, in_specs=placed, out_specs=P(BLK + ULY, None), check_vma=False
    )
```

profile of v0, /device:TPU:6, one launch (start us, length us, event | category | flops | bytes accessed | tf_op | source)
XLA Modules:
  0.0 315.9 jit_solution(15150065198551232142)
XLA Ops:
  6.6 0.7 tile.8
  7.3 1.6 pad_maximum_fusion.1
  9.7 1.5 copy.26
  11.6 1.2 maximum_bitcast_fusion
  12.8 7.4 %all-to-all-start = ((bf16[8,64,1152]{2,1,0:T(8,128)(2,1)}), bf16[8,64,1152]{2,1,0:T(8,128)(2,1)S(1)}, u32[]{:S(2)}, u32[]{:S(2)}) async-start(bf16[8,64,1152]{2,1,0:T(8,128)(2,1)} %maximum_bitcast_fusion), calls=%async_computation | async-start | bytes 2359296 | tf_op jit(solution)/shard_map/all_to_all | solution.py:320
  20.2 5.3 %copy.27 = bf16[384,8,2,384]{3,1,2,0:T(8,128)(2,1)} copy(bf16[384,8,2,384]{3,2,1,0:T(2,128)(2,1)} %bitcast.66) | data formatting | bytes 9437184
  25.5 0.7 fusion.10
  26.2 2.5 select_add_fusion
  28.9 7.3 %all-to-all-done = bf16[8,64,1152]{2,1,0:T(8,128)(2,1)S(1)} async-done(((bf16[8,64,1152]{2,1,0:T(8,128)(2,1)}), bf16[8,64,1152]{2,1,0:T(8,128)(2,1)S(1)}, u32[]{:S(2)}, u32[]{:S(2)}) %all-to-all-start) | async-done | bytes 1179680 | tf_op jit(solution)/shard_map/all_to_all | solution.py:320
  36.3 0.9 collective-permute-start
  37.2 1.9 collective-permute-start.3
  39.1 3.9 %collective-permute-start.4 = (bf16[512,768]{1,0:T(8,128)(2,1)S(1)}, bf16[512,768]{1,0:T(8,128)(2,1)}, u32[]{:S(2)}, u32[]{:S(2)}) collective-permute-start(bf16[512,768]{1,0:T(8,128)(2,1)S(1)} %slice.63.refs_5_.refs_6_.refs_10_), channel_id=1, source_target_pairs={{0,112},{16,0},{32,16},{48,32},{64,48},{80,64},{96,80},{112,96},{1... | collective-permute-start | bytes 2359304 | tf_op jit(solution)/shard_map/ppermute | solution.py:346
  43.1 3.0 collective-permute-done.refs_2_
  46.1 1.7 collective-permute-done.2.refs_4_
  47.8 0.7 copy-done.8
  48.6 7.3 %shard_map.100.refs_9_ = f32[3,2048,256]{2,1,0:T(8,128)} custom-call(s32[1]{0:T(128)} %copy.33.refs_0_, bf16[512,384]{1,0:T(8,128)(2,1)} %copy-done.1, bf16[512,384]{1,0:T(8,128)(2,1)} %copy-done.6, bf16[512,384]{1,0:T(8,128)(2,1)} %copy-done.7, bf16[512,384]{1,0:T(8,128)(2,1)} %copy-done.8, bf16[512,768]{1,0:T(8,128)(2,1)} %copy-done.4, ...), custom_call_target="tpu_custom_call" | custom-call | flops 3145728 | bytes 1048576 | tf_op jit(solution)/shard_map/pallas_call | solution.py:157
  55.9 8.2 %collective-permute-done.3.refs_5_.refs_7_.refs_11_ = bf16[512,768]{1,0:T(8,128)(2,1)S(1)} collective-permute-done((bf16[512,768]{1,0:T(8,128)(2,1)S(1)}, bf16[512,768]{1,0:T(8,128)(2,1)S(1)}, u32[]{:S(2)}, u32[]{:S(2)}) %collective-permute-start.3) | collective-permute-done | bytes 786464 | tf_op jit(solution)/shard_map/ppermute | solution.py:346
  64.1 2.1 fusion
  66.8 3.0 collective-permute-start.6
  69.9 1.6 collective-permute-start.12
  71.5 11.5 %shard_map.101.refs_9_ = f32[3,2048,256]{2,1,0:T(8,128)} custom-call(s32[1]{0:T(128)} %copy.33.refs_0_, bf16[512,384]{1,0:T(8,128)(2,1)} %copy-done.1, bf16[512,384]{1,0:T(8,128)(2,1)} %copy-done.6, bf16[512,384]{1,0:T(8,128)(2,1)} %copy-done.7, bf16[512,384]{1,0:T(8,128)(2,1)} %copy-done.8, bf16[512,768]{1,0:T(8,128)(2,1)} %copy-done.18, ...), custom_call_target="tpu_custom_call" | custom-call | flops 12884901888 | bytes 12582912 | tf_op jit(solution)/shard_map/pallas_call | solution.py:157
  83.1 4.8 %collective-permute-done.5.refs_5_.refs_7_.refs_13_ = bf16[512,768]{1,0:T(8,128)(2,1)} collective-permute-done((bf16[512,768]{1,0:T(8,128)(2,1)}, bf16[512,768]{1,0:T(8,128)(2,1)}, u32[]{:S(2)}, u32[]{:S(2)}) %collective-permute-start.5) | collective-permute-done | bytes 786464 | tf_op jit(solution)/shard_map/ppermute | solution.py:346
  87.9 1.1 collective-permute-start.7
  89.0 2.2 collective-permute-start.8
  91.4 3.3 %convolution_convert_fusion = bf16[32,768]{1,0:T(8,128)(2,1)S(1)} fusion(bf16[3072,768]{1,0:T(8,128)(2,1)} %bitcast.63, f32[32,3072]{1,0:T(8,128)S(1)} %get-tuple-element.58, f32[3072]{0:T(1024)S(1)} %copy-done.15, f32[32]{0:T(128)S(1)} %add_rsqrt_fusion), kind=kOutput, calls=%fused_computation.3 | convolution fusion | flops 151314432 | bytes 5173376 | tf_op jit(solution)/shard_map/dot_general | solution.py:248
  94.8 11.4 %shard_map.102.refs_9_ = f32[3,2048,256]{2,1,0:T(8,128)} custom-call(s32[1]{0:T(128)} %copy.33.refs_0_, bf16[512,384]{1,0:T(8,128)(2,1)} %copy-done.1, bf16[512,384]{1,0:T(8,128)(2,1)} %copy-done.6, bf16[512,384]{1,0:T(8,128)(2,1)} %copy-done.7, bf16[512,384]{1,0:T(8,128)(2,1)} %copy-done.8, ...), custom_call_target="tpu_custom_call" | custom-call | flops 12884901888 | bytes 12582912 | tf_op jit(solution)/shard_map/pallas_call | solution.py:157
  106.2 1.2 collective-permute-start.14
  107.5 4.0 %collective-permute-done.14 = bf16[2,32,768]{2,1,0:T(8,128)(2,1)S(1)} collective-permute-done((bf16[2,32,768]{2,1,0:T(8,128)(2,1)S(1)}, bf16[2,32,768]{2,1,0:T(8,128)(2,1)S(1)}, u32[]{:S(2)}, u32[]{:S(2)}) %collective-permute-start.14) | collective-permute-done | bytes 98336 | tf_op jit(solution)/shard_map/ppermute | solution.py:371
  111.5 0.8 shard_map.103.id_ref
  112.3 0.9 copy-done.3
  113.3 1.8 collective-permute-start.10
  115.5 11.3 %shard_map.104.refs_9_ = f32[3,2048,256]{2,1,0:T(8,128)} custom-call(s32[1]{0:T(128)} %copy.33.refs_0_, bf16[512,384]{1,0:T(8,128)(2,1)} %copy-done.1, bf16[512,384]{1,0:T(8,128)(2,1)} %copy-done.6, bf16[512,384]{1,0:T(8,128)(2,1)} %copy-done.7, bf16[512,384]{1,0:T(8,128)(2,1)} %copy-done.8, bf16[512,768]{1,0:T(8,128)(2,1)} %copy-done.10, ...), custom_call_target="tpu_custom_call" | custom-call | flops 12884901888 | bytes 12582912 | tf_op jit(solution)/shard_map/pallas_call | solution.py:157
  127.6 0.7 copy-done.20
  128.3 135.8 %shard_map.105 = (bf16[1024,384]{1,0:T(8,128)(2,1)}, bf16[1024,384]{1,0:T(8,128)(2,1)}, f32[3,2,1024]{2,1,0:T(2,128)}, f32[3,2,1024]{2,1,0:T(2,128)}) custom-call(s32[1]{0:T(128)} %copy.33.refs_0_, bf16[512,384]{1,0:T(8,128)(2,1)} %copy-done.1, bf16[512,384]{1,0:T(8,128)(2,1)} %copy-done.6, bf16[512,384]{1,0:T(8,128)(2,1)} %copy-done.7, ...), custom_call_target="tpu_custom_call" | custom-call | flops 6442450944 | bytes 12582912 | tf_op jit(solution)/shard_map/pallas_call | solution.py:157
  264.7 1.1 collective-permute-start.17
  266.8 2.0 collective-permute-done.17.lr_x
  268.8 0.8 collective-permute-done.18.lr_far
  269.6 0.6 copy-done.14
  270.5 3.5 %shard_map.106 = bf16[2,512,384]{2,1,0:T(8,128)(2,1)} custom-call(bf16[1024,384]{1,0:T(8,128)(2,1)} %get-tuple-element.47.keep, bf16[1024,384]{1,0:T(8,128)(2,1)} %copy-done.5, f32[3,2,1024]{2,1,0:T(2,128)} %get-tuple-element.49.lr_own, f32[3,2,1024]{2,1,0:T(2,128)} %copy-done.12, f32[3,2,1024]{2,1,0:T(2,128)} %copy-done.13, f32[3,2,1024]{2,1,0:T(2,128)} %copy-done.14, ...), custom_call_target="tpu_custom_call" | custom-call | tf_op jit(solution)/shard_map/pallas_call | solution.py:225
  274.0 17.0 %all_to_all.10.mixed = bf16[8,128,384]{2,1,0:T(8,128)(2,1)S(1)} all-to-all(bf16[8,128,384]{2,1,0:T(8,128)(2,1)} %bitcast.70), channel_id=1, replica_groups=mesh['xl'=2,'z'=8,'c'=2,'y'=4,'xh'=2] {'xl','y'}, dimensions={0} | all-to-all | bytes 1572864 | tf_op jit(solution)/shard_map/all_to_all | solution.py:387
  291.0 3.7 %copy-done = bf16[1536,3072]{1,0:T(8,128)(2,1)S(1)} copy-done((bf16[1536,3072]{1,0:T(8,128)(2,1)S(1)}, bf16[1536,3072]{1,0:T(8,128)(2,1)}, u32[]{:S(2)}) %copy-start) | copy-done | bytes 9437208
  294.7 1.9 shard_map.107
  296.6 1.3 collective-permute-start.19
  297.8 1.9 shard_map.108
  299.7 2.4 collective-permute-start.20
  302.2 3.2 %collective-permute-done.19 = bf16[64,1536]{1,0:T(8,128)(2,1)S(1)} collective-permute-done((bf16[64,1536]{1,0:T(8,128)(2,1)S(1)}, bf16[64,1536]{1,0:T(8,128)(2,1)S(1)}, u32[]{:S(2)}, u32[]{:S(2)}) %collective-permute-start.19) | collective-permute-done | bytes 196640 | tf_op jit(solution)/shard_map/ppermute | solution.py:391
  305.4 2.6 collective-permute-done.20
  308.1 0.8 pad_maximum_fusion
  (88 shorter events, 5.0 us)
Async XLA Ops:
  6.5 57.6 %all-gather.5.cloned.1.call-start = ((), (), s32[]{:S(2)}) async-start(), calls=%async_computation.2 | async-start | bytes 1843200 | tf_op jit(solution)/shard_map/all_gather | solution.py:313
  12.8 23.4 %all-to-all-start = ((bf16[8,64,1152]{2,1,0:T(8,128)(2,1)}), bf16[8,64,1152]{2,1,0:T(8,128)(2,1)S(1)}, u32[]{:S(2)}, u32[]{:S(2)}) async-start(bf16[8,64,1152]{2,1,0:T(8,128)(2,1)} %maximum_bitcast_fusion), calls=%async_computation | async-start | bytes 2359296 | tf_op jit(solution)/shard_map/all_to_all | solution.py:320
  20.2 270.8 %all-gather.7.cloned.1.call-start = ((), (), s32[]{:S(2)}) async-start(), calls=%async_computation.3 | async-start | bytes 11796480 | tf_op jit(solution)/shard_map/all_gather | solution.py:331
  20.2 5.3 %copy-start.17 = (s32[4]{0:T(128)S(1)}, s32[4]{0:T(128)}, u32[]{:S(2)}) copy-start(s32[4]{0:T(128)} %param.13) | copy-start | bytes 52
  20.2 5.9 %copy-start.16 = (s32[512]{0:T(512)S(1)}, s32[512]{0:T(512)}, u32[]{:S(2)}) copy-start(s32[512]{0:T(512)} %param.12) | copy-start | bytes 6148
  36.2 11.6 %copy-start.4 = (bf16[512,768]{1,0:T(8,128)(2,1)}, bf16[512,768]{1,0:T(8,128)(2,1)S(1)}, u32[]{:S(2)}) copy-start(bf16[512,768]{1,0:T(8,128)(2,1)S(1)} %slice.63.refs_5_.refs_6_.refs_10_) | copy-start | bytes 2359300
  36.3 11.5 %copy-start.1 = (bf16[512,384]{1,0:T(8,128)(2,1)}, bf16[512,384]{1,0:T(8,128)(2,1)S(1)}, u32[]{:S(2)}) copy-start(bf16[512,384]{1,0:T(8,128)(2,1)S(1)} %slice.62.refs_1_.q_ref) | copy-start | bytes 1179652
  36.3 9.8 %collective-permute-start = (bf16[512,384]{1,0:T(8,128)(2,1)S(1)}, bf16[512,384]{1,0:T(8,128)(2,1)S(1)}, u32[]{:S(2)}, u32[]{:S(2)}) collective-permute-start(bf16[512,384]{1,0:T(8,128)(2,1)S(1)} %slice.62.refs_1_.q_ref), channel_id=1, source_target_pairs={{0,128},{128,0},{1,129},{129,1},{2,130},{130,2},{3,131},{131,3},{4... | collective-permute-start | bytes 1179656 | tf_op jit(solution)/shard_map/ppermute | solution.py:333
  37.2 26.9 %collective-permute-start.3 = (bf16[512,768]{1,0:T(8,128)(2,1)S(1)}, bf16[512,768]{1,0:T(8,128)(2,1)S(1)}, u32[]{:S(2)}, u32[]{:S(2)}) collective-permute-start(bf16[512,768]{1,0:T(8,128)(2,1)S(1)} %slice.63.refs_5_.refs_6_.refs_10_), channel_id=1, source_target_pairs={{0,16},{16,32},{32,48},{48,64},{64,80},{80,96},{96,112},{112,0},{1... | collective-permute-start | bytes 2359304 | tf_op jit(solution)/shard_map/ppermute | solution.py:346
  39.1 24.9 %collective-permute-start.4 = (bf16[512,768]{1,0:T(8,128)(2,1)S(1)}, bf16[512,768]{1,0:T(8,128)(2,1)}, u32[]{:S(2)}, u32[]{:S(2)}) collective-permute-start(bf16[512,768]{1,0:T(8,128)(2,1)S(1)} %slice.63.refs_5_.refs_6_.refs_10_), channel_id=1, source_target_pairs={{0,112},{16,0},{32,16},{48,32},{64,48},{80,64},{96,80},{112,96},{1... | collective-permute-start | bytes 2359304 | tf_op jit(solution)/shard_map/ppermute | solution.py:346
  43.1 3.0 collective-permute-start.1
  46.1 1.7 copy-start.6
  46.1 1.7 collective-permute-start.2
  46.1 1.7 copy-start.7
  47.8 0.7 copy-start.8
  64.1 2.2 copy-start.18
  66.3 3.4 %collective-permute-start.11 = (f32[2,32,3072]{2,1,0:T(8,128)S(1)}, f32[2,32,3072]{2,1,0:T(8,128)S(1)}, u32[]{:S(2)}, u32[]{:S(2)}) collective-permute-start(f32[2,32,3072]{2,1,0:T(8,128)S(1)} %select_bitcast_fusion), channel_id=1, source_target_pairs={{0,8},{8,0},{1,9},{9,1},{2,10},{10,2},{3,11},{11,3},{4,12},{12,4},... | collective-permute-start | bytes 2359304 | tf_op jit(solution)/shard_map/ppermute | solution.py:362
  66.4 21.5 %collective-permute-start.5 = (bf16[512,768]{1,0:T(8,128)(2,1)}, bf16[512,768]{1,0:T(8,128)(2,1)}, u32[]{:S(2)}, u32[]{:S(2)}) collective-permute-start(bf16[512,768]{1,0:T(8,128)(2,1)} %copy-done.18), channel_id=1, source_target_pairs={{0,16},{16,32},{32,48},{48,64},{64,80},{80,96},{96,112},{112,0},{1... | collective-permute-start | bytes 2359304 | tf_op jit(solution)/shard_map/ppermute | solution.py:346
  66.8 21.1 %collective-permute-start.6 = (bf16[512,768]{1,0:T(8,128)(2,1)}, bf16[512,768]{1,0:T(8,128)(2,1)}, u32[]{:S(2)}, u32[]{:S(2)}) collective-permute-start(bf16[512,768]{1,0:T(8,128)(2,1)} %collective-permute-done.4.refs_6_.refs_8_.refs_12_), channel_id=1, source_target_pairs={{0,112},{16,0},{32,16},{48,32},{64,48},{80,64},{96,80},{112,96},{1... | collective-permute-start | bytes 2359304 | tf_op jit(solution)/shard_map/ppermute | solution.py:346
  69.9 21.2 %copy-start.9 = (bf16[32,3072]{1,0:T(8,128)(2,1)S(1)}, bf16[32,3072]{1,0:T(8,128)(2,1)}, u32[]{:S(2)}) copy-start(bf16[32,3072]{1,0:T(8,128)(2,1)} %param.16) | copy-start | bytes 589828
  69.9 21.2 %collective-permute-start.12 = (f32[32,3072]{1,0:T(8,128)S(1)}, f32[32,3072]{1,0:T(8,128)S(1)}, u32[]{:S(2)}, u32[]{:S(2)}) collective-permute-start(f32[32,3072]{1,0:T(8,128)S(1)} %select_bitcast_fusion.1), channel_id=1, source_target_pairs={{0,128},{128,0},{1,129},{129,1},{2,130},{130,2},{3,131},{131,3},{4... | collective-permute-start | bytes 1179656 | tf_op jit(solution)/shard_map/ppermute | solution.py:365
  83.1 8.3 %copy-start.15 = (f32[3072]{0:T(1024)S(1)}, f32[3072]{0:T(1024)}, u32[]{:S(2)}) copy-start(f32[3072]{0:T(1024)} %param.17) | copy-start | bytes 36868
  87.9 25.3 %collective-permute-start.7 = (bf16[512,768]{1,0:T(8,128)(2,1)}, bf16[512,768]{1,0:T(8,128)(2,1)S(1)}, u32[]{:S(2)}, u32[]{:S(2)}) collective-permute-start(bf16[512,768]{1,0:T(8,128)(2,1)} %collective-permute-done.5.refs_5_.refs_7_.refs_13_), channel_id=1, source_target_pairs={{0,16},{16,32},{32,48},{48,64},{64,80},{80,96},{96,112},{112,0},{1... | collective-permute-start | bytes 2359304 | tf_op jit(solution)/shard_map/ppermute | solution.py:346
  89.0 24.2 %collective-permute-start.8 = (bf16[512,768]{1,0:T(8,128)(2,1)}, bf16[512,768]{1,0:T(8,128)(2,1)S(1)}, u32[]{:S(2)}, u32[]{:S(2)}) collective-permute-start(bf16[512,768]{1,0:T(8,128)(2,1)} %collective-permute-done.6.refs_6_.refs_8_.refs_14_), channel_id=1, source_target_pairs={{0,112},{16,0},{32,16},{48,32},{64,48},{80,64},{96,80},{112,96},{1... | collective-permute-start | bytes 2359304 | tf_op jit(solution)/shard_map/ppermute | solution.py:346
  94.7 16.8 %copy-start.2 = (bf16[512,384]{1,0:T(8,128)(2,1)S(1)}, bf16[512,384]{1,0:T(8,128)(2,1)}, u32[]{:S(2)}) copy-start(bf16[512,384]{1,0:T(8,128)(2,1)} %copy-done.1) | copy-start | bytes 1179652
  94.7 11.5 %collective-permute-start.13 = (bf16[32,768]{1,0:T(8,128)(2,1)S(1)}, bf16[32,768]{1,0:T(8,128)(2,1)S(1)}, u32[]{:S(2)}, u32[]{:S(2)}) collective-permute-start(bf16[32,768]{1,0:T(8,128)(2,1)S(1)} %convolution_convert_fusion), channel_id=1, source_target_pairs={{0,8},{8,0},{1,9},{9,1},{2,10},{10,2},{3,11},{11,3},{4,12},{12,4},... | collective-permute-start | bytes 147464 | tf_op jit(solution)/shard_map/ppermute | solution.py:369
  106.2 5.2 %collective-permute-start.14 = (bf16[2,32,768]{2,1,0:T(8,128)(2,1)S(1)}, bf16[2,32,768]{2,1,0:T(8,128)(2,1)S(1)}, u32[]{:S(2)}, u32[]{:S(2)}) collective-permute-start(bf16[2,32,768]{2,1,0:T(8,128)(2,1)S(1)} %maximum_select_fusion.2), channel_id=1, source_target_pairs={{0,128},{128,0},{1,129},{129,1},{2,130},{130,2},{3,131},{131,3},{4... | collective-permute-start | bytes 294920 | tf_op jit(solution)/shard_map/ppermute | solution.py:371
  112.3 0.9 copy-start.3
  113.2 2.3 copy-start.10
  113.2 2.3 copy-start.11
  113.3 13.5 %collective-permute-start.10 = (bf16[256,768]{1,0:T(8,128)(2,1)S(1)}, bf16[256,768]{1,0:T(8,128)(2,1)S(1)}, u32[]{:S(2)}, u32[]{:S(2)}) collective-permute-start(bf16[256,768]{1,0:T(8,128)(2,1)S(1)} %slice.65), channel_id=1, source_target_pairs={{0,112},{16,0},{32,16},{48,32},{64,48},{80,64},{96,80},{112,96},{1... | collective-permute-start | bytes 1179656 | tf_op jit(solution)/shard_map/ppermute | solution.py:349
  115.2 11.9 %collective-permute-start.9 = (bf16[256,768]{1,0:T(8,128)(2,1)S(1)}, bf16[256,768]{1,0:T(8,128)(2,1)S(1)}, u32[]{:S(2)}, u32[]{:S(2)}) collective-permute-start(bf16[256,768]{1,0:T(8,128)(2,1)S(1)} %slice.64), channel_id=1, source_target_pairs={{0,16},{16,32},{32,48},{48,64},{64,80},{80,96},{96,112},{112,0},{1... | collective-permute-start | bytes 1179656 | tf_op jit(solution)/shard_map/ppermute | solution.py:349
  126.8 0.8 copy-start.19
  127.6 0.8 copy-start.20
  264.1 5.4 %collective-permute-start.15 = (bf16[1024,384]{1,0:T(8,128)(2,1)}, bf16[1024,384]{1,0:T(8,128)(2,1)S(1)}, u32[]{:S(2)}, u32[]{:S(2)}) collective-permute-start(bf16[1024,384]{1,0:T(8,128)(2,1)} %get-tuple-element.48), channel_id=1, source_target_pairs={{0,8},{8,0},{1,9},{9,1},{2,10},{10,2},{3,11},{11,3},{4,12},{12,4},... | collective-permute-start | bytes 2359304 | tf_op jit(solution)/shard_map/ppermute | solution.py:379
  264.2 2.5 collective-permute-start.16
  264.7 4.0 %collective-permute-start.17 = (f32[3,2,1024]{2,1,0:T(2,128)}, f32[3,2,1024]{2,1,0:T(2,128)S(1)}, u32[]{:S(2)}, u32[]{:S(2)}) collective-permute-start(f32[3,2,1024]{2,1,0:T(2,128)} %get-tuple-element.49.lr_own), channel_id=1, source_target_pairs={{0,128},{128,0},{1,129},{129,1},{2,130},{130,2},{3,131},{131,3},{4... | collective-permute-start | bytes 73736 | tf_op jit(solution)/shard_map/ppermute | solution.py:381
  265.8 3.7 %collective-permute-start.18 = (f32[3,2,1024]{2,1,0:T(2,128)}, f32[3,2,1024]{2,1,0:T(2,128)S(1)}, u32[]{:S(2)}, u32[]{:S(2)}) collective-permute-start(f32[3,2,1024]{2,1,0:T(2,128)} %get-tuple-element.50), channel_id=1, source_target_pairs={{0,136},{8,128},{128,8},{136,0},{1,137},{9,129},{129,9},{137,1},{2... | collective-permute-start | bytes 73736 | tf_op jit(solution)/shard_map/ppermute | solution.py:382
  266.8 2.8 copy-start.12
  268.8 0.8 copy-start.13
  269.6 0.6 copy-start.14
  269.6 0.9 copy-start.5
  291.0 3.7 %copy-start = (bf16[1536,3072]{1,0:T(8,128)(2,1)S(1)}, bf16[1536,3072]{1,0:T(8,128)(2,1)}, u32[]{:S(2)}) copy-start(bf16[1536,3072]{1,0:T(8,128)(2,1)} %all-gather.7.cloned.1.call-done) | copy-start | bytes 28311556
  296.6 8.8 %collective-permute-start.19 = (bf16[64,1536]{1,0:T(8,128)(2,1)S(1)}, bf16[64,1536]{1,0:T(8,128)(2,1)S(1)}, u32[]{:S(2)}, u32[]{:S(2)}) collective-permute-start(bf16[64,1536]{1,0:T(8,128)(2,1)S(1)} %get-tuple-element.54), channel_id=1, source_target_pairs={{0,1},{1,0},{2,3},{3,2},{4,5},{5,4},{6,7},{7,6},{8,9},{9,8},{10,11... | collective-permute-start | bytes 589832 | tf_op jit(solution)/shard_map/ppermute | solution.py:391
  299.7 8.3 %collective-permute-start.20 = (bf16[64,1536]{1,0:T(8,128)(2,1)S(1)}, bf16[64,1536]{1,0:T(8,128)(2,1)S(1)}, u32[]{:S(2)}, u32[]{:S(2)}) collective-permute-start(bf16[64,1536]{1,0:T(8,128)(2,1)S(1)} %get-tuple-element.56), channel_id=1, source_target_pairs={{0,1},{1,0},{2,3},{3,2},{4,5},{5,4},{6,7},{7,6},{8,9},{9,8},{10,11... | collective-permute-start | bytes 589832 | tf_op jit(solution)/shard_map/ppermute | solution.py:391
Sparse Core Ops, SparseCore 0:
  9.1 45.7 all-gather.4
  56.8 93.1 all-gather.6
where the time goes:
time: 318 us; the launch traced here: 316 us
  Pallas kernels  185 us (58%)
  waiting for transfers between devices  38.5 us (12%)
  starting transfers between devices  31.7 us (10%)
  blocking collectives  17 us (5%)
  local copies, waits for them, and re-layouts  16.1 us (5%)
  between operations  14.6 us (5%)
  other arithmetic  7.1 us (2%)
  matrix products  5.44 us (2%)
    pallas_call x5, Pallas kernels, attend(): pl.pallas_call(functools.partial(attn_kernel, pieces, marks, marks_all, f...  177 us
    all_to_all x1, blocking collectives, on_device(): mixed = lax.all_to_all(mixed, ('xl', 'y'), 0, 0, tiled=True)  17 us
    unnamed x44, local copies, waits for them, and re-layouts  14.3 us
    ppermute x6, waiting for transfers between devices, on_device(): up, down = (lax.ppermute(up, 'z', right), lax.ppermute(down, 'z', left))  13.1 us
    ppermute x6, starting transfers between devices, on_device(): up, down = (lax.ppermute(up, 'z', right), lax.ppermute(down, 'z', left))  12.4 us
    all_to_all x1, starting transfers between devices, on_device(): got = lax.all_to_all(sent, ULY, 0, 0, tiled=True).reshape(tok_blk, 3 * here)  7.43 us
    all_to_all x1, waiting for transfers between devices, on_device(): got = lax.all_to_all(sent, ULY, 0, 0, tiled=True).reshape(tok_blk, 3 * here)  7.26 us
  transfers between devices with their start and end apart: 24, of which 12 were waited for; matrix products, arithmetic and copies ran while one was open for 6% of the time, Pallas kernels for 58%

commit v1 on v0

--- a/solution.py
+++ b/solution.py
@@ -38,7 +38,7 @@
     v_refs = [refs.pop(0) for _ in range(count)]
     acc_in = None if first else refs.pop(0)
     if last:
-        *shards, keep_ref, send_ref, lr_keep, lr_send, ones, acc_ref, k_buf, v_buf, top_ref = refs
+        *shards, keep_ref, send_ref, lr_keep, lr_send, ones, acc_ref, k_buf, v_buf, top_ref, q_buf = refs
     else:
         acc_ref, ones = refs
     head = pl.program_id(0)
@@ -85,12 +85,23 @@
                 ref[0:1, :] = totals[:, part]
                 ref[1:2, :] = references[:, part]
 
-        totals = acc_ref[:, HEAD : 2 * HEAD].T[0:1, :]
+        def as_row(ref, first_lane):
+            square = (HEAD, HEAD)
+            diagonal = lax.broadcasted_iota(jnp.int32, square, 0) == lax.broadcasted_iota(jnp.int32, square, 1)
+            parts = []
+            for at in range(0, rows_here, HEAD):
+                block = ref[at : at + HEAD, first_lane : first_lane + HEAD]
+                parts.append(jnp.sum(jnp.where(diagonal, block, 0.0), axis=0, keepdims=True))
+            return jnp.concatenate(parts, axis=1)
+
+        totals = as_row(acc_ref, HEAD)
         write(totals, jnp.zeros_like(totals))
         good = jnp.min(jnp.where((totals >= 2.0**-60) & (totals <= 2.0**100), 1.0, 0.0)) > 0.5
 
         @pl.when(jnp.logical_not(good))
         def _():
+            for start in range(0, rows_here, sub):
+                q_buf[start : start + sub, :] = split(start)
             acc_ref[...] = jnp.zeros_like(acc_ref)
             top_ref[...] = jnp.full_like(top_ref, -1e30)
             for i, shard in enumerate(shards):
@@ -99,20 +110,25 @@
                 value_at = pl.multiple_of(shard.shape[1] // 2 + head * HEAD, HEAD)
                 pltpu.sync_copy(shard.at[:, pl.ds(key_at, HEAD)], k_buf.at[here, :])
                 pltpu.sync_copy(shard.at[:, pl.ds(value_at, HEAD)], v_buf.at[here, :])
-                for start in range(0, rows_here, sub):
-                    part = slice(start, start + sub)
-                    scores = score(split(start), k_buf[here, :])
+                limit = usable(text_count[0], marks_all[i])
+
+                @pl.loop(0, rows_here // sub)
+                def _(n):
+                    part = pl.ds(pl.multiple_of(n * sub, sub), sub)
+                    scores = score(q_buf[part, :], k_buf[here, :])
                     key = lax.broadcasted_iota(jnp.int32, scores.shape, 1)
-                    scores = jnp.where(key < usable(text_count[0], marks_all[i]), scores, -1e30)
-                    old = top_ref[part, 0:1]
+                    scores = jnp.where(key < limit, scores, -1e30)
+                    old = top_ref[part, :]
                     new = jnp.maximum(old, jnp.max(scores, axis=1, keepdims=True))
-                    p = jnp.exp2(scores - new).astype(bf16)
+                    p = jnp.exp2(scores - new[:, 0:1]).astype(bf16)
                     v = v_buf[here, :]
                     v = jnp.concatenate([v, jnp.ones_like(v)], axis=1)
                     added = jnp.dot(p, v, preferred_element_type=f32)
-                    acc_ref[part, :] = acc_ref[part, :] * jnp.exp2(old - new) + added
-                    top_ref[part, :] = jnp.broadcast_to(new, (sub, HEAD))
-            write(acc_ref[:, HEAD : 2 * HEAD].T[0:1, :], top_ref[...].T[0:1, :])
+                    factor = jnp.exp2(old - new)
+                    acc_ref[part, :] = acc_ref[part, :] * jnp.concatenate([factor, factor], axis=1) + added
+                    top_ref[part, :] = new
+
+            write(as_row(acc_ref, HEAD), as_row(top_ref, 0))
 
 
 def attend(text_count, queries, shards, acc, everything=None, sub=SUB):
@@ -150,6 +166,7 @@
             pltpu.VMEM((keys, HEAD), bf16),
             pltpu.VMEM((keys, HEAD), bf16),
             pltpu.VMEM((rows, HEAD), f32),
+            pltpu.VMEM((rows, 2 * HEAD), bf16),
         ]
     else:
         out_specs = acc_block
@@ -199,6 +216,8 @@
     slot = pl.program_id(0)
     tokens, width = keep.shape
     place = lax.rem(lax.axis_index("xl") + slot, 2)
+    square = (HEAD, HEAD)
+    diagonal = lax.broadcasted_iota(jnp.int32, square, 0) == lax.broadcasted_iota(jnp.int32, square, 1)
     for h in range(width // HEAD):
         refs = [r[h, 1:2, :] for r in (lr_own, lr_core, lr_x, lr_far)]
         sums = [r[h, 0:1, :] for r in (lr_own, lr_core, lr_x, lr_far)]
@@ -206,14 +225,20 @@
         weight = [jnp.exp2(r - top) for r in refs]
         total = sum(w * s for w, s in zip(weight, sums))
 
-        def column(row):
-            return jnp.broadcast_to(row, (HEAD, tokens)).T
-
-        cols = slice(h * HEAD, (h + 1) * HEAD)
-        value = keep[:, cols].astype(f32) * column(weight[0] / total)
-        value = value + recv[:, cols].astype(f32) * column(weight[1] / total)
-        value = value + jnp.where(slot == 0, id_ref[:, cols], 0.0)
-        out_ref[place, :, cols] = value.astype(bf16)
+        scales = [weight[0] / total, weight[1] / total]
+        for at in range(0, tokens, HEAD):
+            rows, cols = slice(at, at + HEAD), slice(h * HEAD, (h + 1) * HEAD)
+            left, right = [], []
+            for scale, data in zip(scales, (keep, recv)):
+                exact = jnp.where(diagonal, scale[:, rows], 0.0)
+                high = exact.astype(bf16)
+                left += [high, (exact - high.astype(f32)).astype(bf16)]
+                right += [data[rows, cols]] * 2
+            value = jnp.dot(
+                jnp.concatenate(left, axis=1), jnp.concatenate(right, axis=0), preferred_element_type=f32
+            )
+            value = value + jnp.where(slot == 0, id_ref[rows, cols], 0.0)
+            out_ref[place, rows, cols] = value.astype(bf16)
 
 
 def combine(keep, recv, lr_keep, lr_core, lr_x, lr_far, idpart):
@@ -228,7 +253,7 @@
         in_specs=[data, data, near, near, cross, cross, pl.BlockSpec((tokens, width), lambda s: (0, 0))],
         out_specs=pl.BlockSpec((2, tokens, width), lambda s: (0, 0, 0)),
         out_shape=jax.ShapeDtypeStruct((2, tokens, width), bf16),
-        compiler_params=pltpu.CompilerParams(vmem_limit_bytes=60 * 2**20),
+        compiler_params=pltpu.CompilerParams(vmem_limit_bytes=16 * 2**20),
     )(keep, recv, lr_keep, lr_core, lr_x, lr_far, idpart)
 
 
@@ -350,30 +375,31 @@
             arriving = [(up, (end, 0, half)), (down, (end, half, half))]
         acc = attend(text_count, queries, pending, acc)
         if step == 1:
-            up, down, acc, gathered = lax.optimization_barrier((up, down, acc, gathered))
-        elif step < end:
             up, down, acc = lax.optimization_barrier((up, down, acc))
+        elif step == 2:
+            acc, gathered = lax.optimization_barrier((acc, gathered))
+            terms = pooled_terms(gathered, width).reshape(2, 2, IDTOK, width)
+            own = jnp.where(my_c == 0, terms[:, 0], terms[:, 1])
+            other = jnp.where(my_c == 0, terms[:, 1], terms[:, 0])
+            up, down, acc, own, other = lax.optimization_barrier((up, down, acc, own, other))
+            terms = own + lax.ppermute(other, "c", SWAP)
+            pooled = jnp.where(my_xl == 0, terms[0], terms[1])
+            pooled = pooled + lax.ppermute(jnp.where(my_xl == 0, terms[1], terms[0]), "xl", SWAP)
+        elif step == end - 1:
+            id_rows = identity_rows(pooled, latents, id_gain, flat_weight)
+            up, down, acc, id_rows = lax.optimization_barrier((up, down, acc, id_rows))
         if step < end:
             arriving = [(up, arriving[0][1]), (down, arriving[1][1])]
         whole += pending
         pending = arriving
     whole += pending
-    terms = pooled_terms(gathered, width).reshape(2, 2, IDTOK, width)
-    terms = jnp.where(my_c == 0, terms[:, 0], terms[:, 1]) + lax.ppermute(
-        jnp.where(my_c == 0, terms[:, 1], terms[:, 0]), "c", SWAP
-    )
-    pooled = jnp.where(my_xl == 0, terms[0], terms[1]) + lax.ppermute(
-        jnp.where(my_xl == 0, terms[1], terms[0]), "xl", SWAP
-    )
-    id_rows = identity_rows(pooled, latents, id_gain, flat_weight)
     id_core = lax.ppermute(id_rows, "c", SWAP)
     id_pair = jnp.where(my_c == 0, jnp.stack([id_rows, id_core]), jnp.stack([id_core, id_rows]))
+    id_pair, acc = lax.optimization_barrier((id_pair, acc))
     id_x = lax.ppermute(id_pair, "xl", SWAP)
     id_kv = jnp.where(my_xl == 0, jnp.stack([id_pair, id_x]), jnp.stack([id_x, id_pair]))
     id_kv = id_kv.reshape(SUBJ * IDTOK, 2 * here)
     idpart = id_attend(q_own, id_kv, match)
-
-    idpart, acc = lax.optimization_barrier((idpart, acc))
     keep, send, lr_keep, lr_send = attend(text_count, queries, pending, acc, everything=whole)
 
     recv = lax.ppermute(send, "c", SWAP)

time: 318 us -> 386 us (1.21)
  Pallas kernels: 185 us -> 259 us
  waiting for transfers between devices: 38.5 us -> 31.2 us
    pallas_call x5, Pallas kernels: 177 us -> 253 us  [attend(): pl.pallas_call(functools.partial(attn_kernel, pieces, marks, marks_all, f...]
    unnamed x44 -> x38, local copies, waits for them, and re-layouts: 14.3 us -> 14.3 us
  transfers between devices with their start and end apart: 24 -> 24, of which waited for: 12 -> 9; matrix products, arithmetic and copies ran while one was open for 6% -> 5% of each run, Pallas kernels for 58% -> 67%
where the time goes in v1:
time: 386 us; the launch traced here: 383 us
  Pallas kernels  259 us (67%)
  starting transfers between devices  33 us (9%)
  waiting for transfers between devices  31.2 us (8%)
  local copies, waits for them, and re-layouts  17.1 us (4%)
  blocking collectives  16.5 us (4%)
  between operations  14.4 us (4%)
  other arithmetic  6.99 us (2%)
  matrix products  5.22 us (1%)
    pallas_call x5, Pallas kernels, attend(): pl.pallas_call(functools.partial(attn_kernel, pieces, marks, marks_all, f...  253 us
    all_to_all x1, blocking collectives, on_device(): mixed = lax.all_to_all(mixed, ('xl', 'y'), 0, 0, tiled=True)  16.5 us
    unnamed x38, local copies, waits for them, and re-layouts  14.3 us
    ppermute x6, starting transfers between devices, on_device(): up, down = (lax.ppermute(up, 'z', right), lax.ppermute(down, 'z', left))  12.3 us
    ppermute x6, waiting for transfers between devices, on_device(): up, down = (lax.ppermute(up, 'z', right), lax.ppermute(down, 'z', left))  12 us
  transfers between devices with their start and end apart: 24, of which 9 were waited for; matrix products, arithmetic and copies ran while one was open for 5% of the time, Pallas kernels for 67%

profile of v1, /device:TPU:6, one launch (start us, length us, event | category | flops | bytes accessed | tf_op | source)
XLA Modules:
  0.0 383.5 jit_solution(10222855441456894757)
XLA Ops:
  6.6 0.7 tile.8
  7.3 1.6 pad_maximum_fusion.1
  9.6 1.5 copy.26
  11.5 1.2 maximum_bitcast_fusion
  12.7 7.4 %all-to-all-start = ((bf16[8,64,1152]{2,1,0:T(8,128)(2,1)}), bf16[8,64,1152]{2,1,0:T(8,128)(2,1)S(1)}, u32[]{:S(2)}, u32[]{:S(2)}) async-start(bf16[8,64,1152]{2,1,0:T(8,128)(2,1)} %maximum_bitcast_fusion), calls=%async_computation | async-start | bytes 2359296 | tf_op jit(solution)/shard_map/all_to_all | solution.py:345
  20.2 5.4 %copy.27 = bf16[384,8,2,384]{3,1,2,0:T(8,128)(2,1)} copy(bf16[384,8,2,384]{3,2,1,0:T(2,128)(2,1)} %bitcast.65) | data formatting | bytes 9437184
  26.2 2.4 select_add_fusion
  28.8 7.3 %all-to-all-done = bf16[8,64,1152]{2,1,0:T(8,128)(2,1)S(1)} async-done(((bf16[8,64,1152]{2,1,0:T(8,128)(2,1)}), bf16[8,64,1152]{2,1,0:T(8,128)(2,1)S(1)}, u32[]{:S(2)}, u32[]{:S(2)}) %all-to-all-start) | async-done | bytes 1179680 | tf_op jit(solution)/shard_map/all_to_all | solution.py:345
  36.3 0.9 collective-permute-start
  37.2 1.9 collective-permute-start.3
  39.1 3.9 %collective-permute-start.4 = (bf16[512,768]{1,0:T(8,128)(2,1)S(1)}, bf16[512,768]{1,0:T(8,128)(2,1)}, u32[]{:S(2)}, u32[]{:S(2)}) collective-permute-start(bf16[512,768]{1,0:T(8,128)(2,1)S(1)} %slice.63.refs_5_.refs_6_.refs_10_), channel_id=1, source_target_pairs={{0,112},{16,0},{32,16},{48,32},{64,48},{80,64},{96,80},{112,96},{1... | collective-permute-start | bytes 2359304 | tf_op jit(solution)/shard_map/ppermute | solution.py:371
  43.0 3.0 collective-permute-done.refs_2_
  46.0 1.7 collective-permute-done.2.refs_4_
  47.8 0.7 copy-done.8
  48.5 7.4 %shard_map.100.refs_9_ = f32[3,2048,256]{2,1,0:T(8,128)} custom-call(s32[1]{0:T(128)} %copy.33.refs_0_, bf16[512,384]{1,0:T(8,128)(2,1)} %copy-done.1, bf16[512,384]{1,0:T(8,128)(2,1)} %copy-done.6, bf16[512,384]{1,0:T(8,128)(2,1)} %copy-done.7, bf16[512,384]{1,0:T(8,128)(2,1)} %copy-done.8, bf16[512,768]{1,0:T(8,128)(2,1)} %copy-done.5, ...), custom_call_target="tpu_custom_call" | custom-call | flops 3145728 | bytes 1048576 | tf_op jit(solution)/shard_map/pallas_call | solution.py:174
  55.9 8.1 %collective-permute-done.3.refs_5_.refs_7_.refs_11_ = bf16[512,768]{1,0:T(8,128)(2,1)S(1)} collective-permute-done((bf16[512,768]{1,0:T(8,128)(2,1)S(1)}, bf16[512,768]{1,0:T(8,128)(2,1)S(1)}, u32[]{:S(2)}, u32[]{:S(2)}) %collective-permute-start.3) | collective-permute-done | bytes 786464 | tf_op jit(solution)/shard_map/ppermute | solution.py:371
  64.6 2.7 collective-permute-start.6
  67.3 12.0 %shard_map.101.refs_9_ = f32[3,2048,256]{2,1,0:T(8,128)} custom-call(s32[1]{0:T(128)} %copy.33.refs_0_, bf16[512,384]{1,0:T(8,128)(2,1)} %copy-done.1, bf16[512,384]{1,0:T(8,128)(2,1)} %copy-done.6, bf16[512,384]{1,0:T(8,128)(2,1)} %copy-done.7, bf16[512,384]{1,0:T(8,128)(2,1)} %copy-done.8, bf16[512,768]{1,0:T(8,128)(2,1)} %copy-done.14, ...), custom_call_target="tpu_custom_call" | custom-call | flops 12884901888 | bytes 12582912 | tf_op jit(solution)/shard_map/pallas_call | solution.py:174
  79.3 1.9 fusion
  81.3 2.7 collective-permute-done.5.refs_5_.refs_7_.refs_13_
  83.9 0.9 copy-done.15
  84.8 0.8 collective-permute-start.7
  85.6 2.5 collective-permute-start.8
  88.2 1.4 collective-permute-start.10
  89.6 11.4 %shard_map.102.refs_9_ = f32[3,2048,256]{2,1,0:T(8,128)} custom-call(s32[1]{0:T(128)} %copy.33.refs_0_, bf16[512,384]{1,0:T(8,128)(2,1)} %copy-done.1, bf16[512,384]{1,0:T(8,128)(2,1)} %copy-done.6, bf16[512,384]{1,0:T(8,128)(2,1)} %copy-done.7, bf16[512,384]{1,0:T(8,128)(2,1)} %copy-done.8, bf16[512,768]{1,0:T(8,128)(2,1)} %copy-done.15, ...), custom_call_target="tpu_custom_call" | custom-call | flops 12884901888 | bytes 12582912 | tf_op jit(solution)/shard_map/pallas_call | solution.py:174
  101.7 3.4 convolution_convert_fusion
  105.0 1.2 collective-permute-done.7.refs_5_.refs_7_.refs_15_
  106.3 1.2 collective-permute-start.11
  107.4 1.0 slice.71
  108.5 2.4 collective-permute-start.12
  110.9 11.2 %shard_map.103.refs_9_ = f32[3,2048,256]{2,1,0:T(8,128)} custom-call(s32[1]{0:T(128)} %copy.33.refs_0_, bf16[512,384]{1,0:T(8,128)(2,1)} %copy-done.1, bf16[512,384]{1,0:T(8,128)(2,1)} %copy-done.6, bf16[512,384]{1,0:T(8,128)(2,1)} %copy-done.7, bf16[512,384]{1,0:T(8,128)(2,1)} %copy-done.8, bf16[512,768]{1,0:T(8,128)(2,1)} %copy-done.10, ...), custom_call_target="tpu_custom_call" | custom-call | flops 12884901888 | bytes 12582912 | tf_op jit(solution)/shard_map/pallas_call | solution.py:174
  122.2 0.8 copy-done.16
  123.0 0.8 copy-done.17
  123.8 211.2 %shard_map.104 = (bf16[1024,384]{1,0:T(8,128)(2,1)}, bf16[1024,384]{1,0:T(8,128)(2,1)}, f32[3,2,1024]{2,1,0:T(2,128)}, f32[3,2,1024]{2,1,0:T(2,128)}) custom-call(s32[1]{0:T(128)} %copy.33.refs_0_, bf16[512,384]{1,0:T(8,128)(2,1)} %copy-done.1, bf16[512,384]{1,0:T(8,128)(2,1)} %copy-done.6, bf16[512,384]{1,0:T(8,128)(2,1)} %copy-done.7, ...), custom_call_target="tpu_custom_call" | custom-call | flops 6442450944 | bytes 12582912 | tf_op jit(solution)/shard_map/pallas_call | solution.py:174
  335.2 1.3 collective-permute-start.18
  337.4 1.3 collective-permute-start.16
  338.7 2.1 collective-permute-done.18
  340.8 0.8 shard_map.105.id_ref
  341.7 1.3 shard_map.106
  343.0 16.5 %all_to_all.10.mixed = bf16[8,128,384]{2,1,0:T(8,128)(2,1)S(1)} all-to-all(bf16[8,128,384]{2,1,0:T(8,128)(2,1)S(1)} %bitcast.61), channel_id=1, replica_groups=mesh['xl'=2,'z'=8,'c'=2,'y'=4,'xh'=2] {'xl','y'}, dimensions={0} | all-to-all | bytes 1572864 | tf_op jit(solution)/shard_map/all_to_all | solution.py:413
  359.5 3.7 copy-done
  363.2 1.9 shard_map.107
  365.1 1.3 collective-permute-start.19
  366.3 1.9 shard_map.108
  368.2 2.4 collective-permute-start.20
  370.6 3.0 collective-permute-done.19
  373.7 2.1 collective-permute-done.20
  375.8 0.8 pad_maximum_fusion
  (81 shorter events, 4.2 us)
Async XLA Ops:
  6.5 72.7 %all-gather.5.cloned.1.call-start = ((), (), s32[]{:S(2)}) async-start(), calls=%async_computation.2 | async-start | bytes 1843200 | tf_op jit(solution)/shard_map/all_gather | solution.py:338
  12.7 23.4 %all-to-all-start = ((bf16[8,64,1152]{2,1,0:T(8,128)(2,1)}), bf16[8,64,1152]{2,1,0:T(8,128)(2,1)S(1)}, u32[]{:S(2)}, u32[]{:S(2)}) async-start(bf16[8,64,1152]{2,1,0:T(8,128)(2,1)} %maximum_bitcast_fusion), calls=%async_computation | async-start | bytes 2359296 | tf_op jit(solution)/shard_map/all_to_all | solution.py:345
  20.2 339.3 %all-gather.7.cloned.1.call-start = ((), (), s32[]{:S(2)}) async-start(), calls=%async_computation.3 | async-start | bytes 11796480 | tf_op jit(solution)/shard_map/all_gather | solution.py:356
  20.2 5.4 %copy-start.13 = (s32[4]{0:T(128)S(1)}, s32[4]{0:T(128)}, u32[]{:S(2)}) copy-start(s32[4]{0:T(128)} %param.13) | copy-start | bytes 52
  20.2 6.0 %copy-start.12 = (s32[512]{0:T(512)S(1)}, s32[512]{0:T(512)}, u32[]{:S(2)}) copy-start(s32[512]{0:T(512)} %param.12) | copy-start | bytes 6148
  36.2 11.6 %copy-start.5 = (bf16[512,768]{1,0:T(8,128)(2,1)}, bf16[512,768]{1,0:T(8,128)(2,1)S(1)}, u32[]{:S(2)}) copy-start(bf16[512,768]{1,0:T(8,128)(2,1)S(1)} %slice.63.refs_5_.refs_6_.refs_10_) | copy-start | bytes 2359300
  36.3 11.5 %copy-start.1 = (bf16[512,384]{1,0:T(8,128)(2,1)}, bf16[512,384]{1,0:T(8,128)(2,1)S(1)}, u32[]{:S(2)}) copy-start(bf16[512,384]{1,0:T(8,128)(2,1)S(1)} %slice.62.refs_1_.q_ref) | copy-start | bytes 1179652
  36.3 9.8 %collective-permute-start = (bf16[512,384]{1,0:T(8,128)(2,1)S(1)}, bf16[512,384]{1,0:T(8,128)(2,1)S(1)}, u32[]{:S(2)}, u32[]{:S(2)}) collective-permute-start(bf16[512,384]{1,0:T(8,128)(2,1)S(1)} %slice.62.refs_1_.q_ref), channel_id=1, source_target_pairs={{0,128},{128,0},{1,129},{129,1},{2,130},{130,2},{3,131},{131,3},{4... | collective-permute-start | bytes 1179656 | tf_op jit(solution)/shard_map/ppermute | solution.py:358
  37.2 26.9 %collective-permute-start.3 = (bf16[512,768]{1,0:T(8,128)(2,1)S(1)}, bf16[512,768]{1,0:T(8,128)(2,1)S(1)}, u32[]{:S(2)}, u32[]{:S(2)}) collective-permute-start(bf16[512,768]{1,0:T(8,128)(2,1)S(1)} %slice.63.refs_5_.refs_6_.refs_10_), channel_id=1, source_target_pairs={{0,16},{16,32},{32,48},{48,64},{64,80},{80,96},{96,112},{112,0},{1... | collective-permute-start | bytes 2359304 | tf_op jit(solution)/shard_map/ppermute | solution.py:371
  39.1 24.9 %collective-permute-start.4 = (bf16[512,768]{1,0:T(8,128)(2,1)S(1)}, bf16[512,768]{1,0:T(8,128)(2,1)}, u32[]{:S(2)}, u32[]{:S(2)}) collective-permute-start(bf16[512,768]{1,0:T(8,128)(2,1)S(1)} %slice.63.refs_5_.refs_6_.refs_10_), channel_id=1, source_target_pairs={{0,112},{16,0},{32,16},{48,32},{64,48},{80,64},{96,80},{112,96},{1... | collective-permute-start | bytes 2359304 | tf_op jit(solution)/shard_map/ppermute | solution.py:371
  43.0 3.0 collective-permute-start.1
  46.0 1.7 copy-start.6
  46.0 1.7 collective-permute-start.2
  46.0 1.7 copy-start.7
  47.8 0.7 copy-start.8
  64.0 3.2 copy-start.14
  64.0 19.9 %collective-permute-start.5 = (bf16[512,768]{1,0:T(8,128)(2,1)S(1)}, bf16[512,768]{1,0:T(8,128)(2,1)S(1)}, u32[]{:S(2)}, u32[]{:S(2)}) collective-permute-start(bf16[512,768]{1,0:T(8,128)(2,1)S(1)} %collective-permute-done.3.refs_5_.refs_7_.refs_11_), channel_id=1, source_target_pairs={{0,16},{16,32},{32,48},{48,64},{64,80},{80,96},{96,112},{112,0},{1... | collective-permute-start | bytes 2359304 | tf_op jit(solution)/shard_map/ppermute | solution.py:371
  64.6 19.4 %collective-permute-start.6 = (bf16[512,768]{1,0:T(8,128)(2,1)}, bf16[512,768]{1,0:T(8,128)(2,1)}, u32[]{:S(2)}, u32[]{:S(2)}) collective-permute-start(bf16[512,768]{1,0:T(8,128)(2,1)} %collective-permute-done.4.refs_6_.refs_8_.refs_12_), channel_id=1, source_target_pairs={{0,112},{16,0},{32,16},{48,32},{64,48},{80,64},{96,80},{112,96},{1... | collective-permute-start | bytes 2359304 | tf_op jit(solution)/shard_map/ppermute | solution.py:371
  83.9 0.9 copy-start.15
  84.8 3.2 collective-permute-start.9
  84.8 21.4 %collective-permute-start.7 = (bf16[512,768]{1,0:T(8,128)(2,1)}, bf16[512,768]{1,0:T(8,128)(2,1)S(1)}, u32[]{:S(2)}, u32[]{:S(2)}) collective-permute-start(bf16[512,768]{1,0:T(8,128)(2,1)} %copy-done.15), channel_id=1, source_target_pairs={{0,16},{16,32},{32,48},{48,64},{64,80},{80,96},{96,112},{112,0},{1... | collective-permute-start | bytes 2359304 | tf_op jit(solution)/shard_map/ppermute | solution.py:371
  85.6 20.6 %collective-permute-start.8 = (bf16[512,768]{1,0:T(8,128)(2,1)}, bf16[512,768]{1,0:T(8,128)(2,1)}, u32[]{:S(2)}, u32[]{:S(2)}) collective-permute-start(bf16[512,768]{1,0:T(8,128)(2,1)} %collective-permute-done.6.refs_6_.refs_8_.refs_14_), channel_id=1, source_target_pairs={{0,112},{16,0},{32,16},{48,32},{64,48},{80,64},{96,80},{112,96},{1... | collective-permute-start | bytes 2359304 | tf_op jit(solution)/shard_map/ppermute | solution.py:371
  88.2 12.8 %copy-start.9 = (bf16[32,3072]{1,0:T(8,128)(2,1)S(1)}, bf16[32,3072]{1,0:T(8,128)(2,1)}, u32[]{:S(2)}) copy-start(bf16[32,3072]{1,0:T(8,128)(2,1)} %param.16) | copy-start | bytes 589828
  88.2 12.7 %collective-permute-start.10 = (f32[32,3072]{1,0:T(8,128)S(1)}, f32[32,3072]{1,0:T(8,128)S(1)}, u32[]{:S(2)}, u32[]{:S(2)}) collective-permute-start(f32[32,3072]{1,0:T(8,128)S(1)} %select_bitcast_fusion.2), channel_id=1, source_target_pairs={{0,128},{128,0},{1,129},{129,1},{2,130},{130,2},{3,131},{131,3},{4... | collective-permute-start | bytes 1179656 | tf_op jit(solution)/shard_map/ppermute | solution.py:387
  101.0 0.7 copy-start.11
  106.2 4.7 %copy-start.10 = (bf16[512,768]{1,0:T(8,128)(2,1)}, bf16[512,768]{1,0:T(8,128)(2,1)S(1)}, u32[]{:S(2)}) copy-start(bf16[512,768]{1,0:T(8,128)(2,1)S(1)} %collective-permute-done.7.refs_5_.refs_7_.refs_15_) | copy-start | bytes 2359300
  106.2 15.9 %collective-permute-start.13 = (bf16[32,768]{1,0:T(8,128)(2,1)S(1)}, bf16[32,768]{1,0:T(8,128)(2,1)S(1)}, u32[]{:S(2)}, u32[]{:S(2)}) collective-permute-start(bf16[32,768]{1,0:T(8,128)(2,1)S(1)} %convolution_convert_fusion), channel_id=1, source_target_pairs={{0,8},{8,0},{1,9},{9,1},{2,10},{10,2},{3,11},{11,3},{4,12},{12,4},... | collective-permute-start | bytes 147464 | tf_op jit(solution)/shard_map/ppermute | solution.py:396
  106.3 15.9 %collective-permute-start.11 = (bf16[256,768]{1,0:T(8,128)(2,1)S(1)}, bf16[256,768]{1,0:T(8,128)(2,1)S(1)}, u32[]{:S(2)}, u32[]{:S(2)}) collective-permute-start(bf16[256,768]{1,0:T(8,128)(2,1)S(1)} %slice.70), channel_id=1, source_target_pairs={{0,16},{16,32},{32,48},{48,64},{64,80},{80,96},{96,112},{112,0},{1... | collective-permute-start | bytes 1179656 | tf_op jit(solution)/shard_map/ppermute | solution.py:374
  108.5 13.7 %collective-permute-start.12 = (bf16[256,768]{1,0:T(8,128)(2,1)S(1)}, bf16[256,768]{1,0:T(8,128)(2,1)S(1)}, u32[]{:S(2)}, u32[]{:S(2)}) collective-permute-start(bf16[256,768]{1,0:T(8,128)(2,1)S(1)} %slice.71), channel_id=1, source_target_pairs={{0,112},{16,0},{32,16},{48,32},{64,48},{80,64},{96,80},{112,96},{1... | collective-permute-start | bytes 1179656 | tf_op jit(solution)/shard_map/ppermute | solution.py:374
  122.2 218.7 %copy-start.2 = (bf16[512,384]{1,0:T(8,128)(2,1)S(1)}, bf16[512,384]{1,0:T(8,128)(2,1)}, u32[]{:S(2)}) copy-start(bf16[512,384]{1,0:T(8,128)(2,1)} %copy-done.1) | copy-start | bytes 1179652
  122.2 0.8 copy-start.16
  123.0 0.8 copy-start.17
  335.0 6.6 %copy-start.3 = (bf16[1024,384]{1,0:T(8,128)(2,1)S(1)}, bf16[1024,384]{1,0:T(8,128)(2,1)}, u32[]{:S(2)}) copy-start(bf16[1024,384]{1,0:T(8,128)(2,1)} %get-tuple-element.54.keep) | copy-start | bytes 2359300
  335.0 6.6 %copy-start.4 = (f32[3,2,1024]{2,1,0:T(2,128)S(1)}, f32[3,2,1024]{2,1,0:T(2,128)}, u32[]{:S(2)}) copy-start(f32[3,2,1024]{2,1,0:T(2,128)} %get-tuple-element.56.lr_own) | copy-start | bytes 73732
  335.1 6.6 %collective-permute-start.14 = (bf16[1024,384]{1,0:T(8,128)(2,1)}, bf16[1024,384]{1,0:T(8,128)(2,1)S(1)}, u32[]{:S(2)}, u32[]{:S(2)}) collective-permute-start(bf16[1024,384]{1,0:T(8,128)(2,1)} %get-tuple-element.55), channel_id=1, source_target_pairs={{0,8},{8,0},{1,9},{9,1},{2,10},{10,2},{3,11},{11,3},{4,12},{12,4},... | collective-permute-start | bytes 2359304 | tf_op jit(solution)/shard_map/ppermute | solution.py:405
  335.2 5.6 %collective-permute-start.18 = (bf16[2,32,768]{2,1,0:T(8,128)(2,1)S(1)}, bf16[2,32,768]{2,1,0:T(8,128)(2,1)S(1)}, u32[]{:S(2)}, u32[]{:S(2)}) collective-permute-start(bf16[2,32,768]{2,1,0:T(8,128)(2,1)S(1)} %maximum_select_fusion.1), channel_id=1, source_target_pairs={{0,128},{128,0},{1,129},{129,1},{2,130},{130,2},{3,131},{131,3},{4... | collective-permute-start | bytes 294920 | tf_op jit(solution)/shard_map/ppermute | solution.py:399
  336.6 5.1 %collective-permute-start.15 = (f32[3,2,1024]{2,1,0:T(2,128)}, f32[3,2,1024]{2,1,0:T(2,128)S(1)}, u32[]{:S(2)}, u32[]{:S(2)}) collective-permute-start(f32[3,2,1024]{2,1,0:T(2,128)} %get-tuple-element.57), channel_id=1, source_target_pairs={{0,8},{8,0},{1,9},{9,1},{2,10},{10,2},{3,11},{11,3},{4,12},{12,4},... | collective-permute-start | bytes 73736 | tf_op jit(solution)/shard_map/ppermute | solution.py:406
  336.7 4.9 %collective-permute-start.17 = (f32[3,2,1024]{2,1,0:T(2,128)}, f32[3,2,1024]{2,1,0:T(2,128)S(1)}, u32[]{:S(2)}, u32[]{:S(2)}) collective-permute-start(f32[3,2,1024]{2,1,0:T(2,128)} %get-tuple-element.57), channel_id=1, source_target_pairs={{0,136},{8,128},{128,8},{136,0},{1,137},{9,129},{129,9},{137,1},{2... | collective-permute-start | bytes 73736 | tf_op jit(solution)/shard_map/ppermute | solution.py:408
  337.4 4.3 %collective-permute-start.16 = (f32[3,2,1024]{2,1,0:T(2,128)}, f32[3,2,1024]{2,1,0:T(2,128)S(1)}, u32[]{:S(2)}, u32[]{:S(2)}) collective-permute-start(f32[3,2,1024]{2,1,0:T(2,128)} %get-tuple-element.56.lr_own), channel_id=1, source_target_pairs={{0,128},{128,0},{1,129},{129,1},{2,130},{130,2},{3,131},{131,3},{4... | collective-permute-start | bytes 73736 | tf_op jit(solution)/shard_map/ppermute | solution.py:407
  359.5 3.7 copy-start
  365.1 8.6 %collective-permute-start.19 = (bf16[64,1536]{1,0:T(8,128)(2,1)S(1)}, bf16[64,1536]{1,0:T(8,128)(2,1)S(1)}, u32[]{:S(2)}, u32[]{:S(2)}) collective-permute-start(bf16[64,1536]{1,0:T(8,128)(2,1)S(1)} %get-tuple-element.62), channel_id=1, source_target_pairs={{0,1},{1,0},{2,3},{3,2},{4,5},{5,4},{6,7},{7,6},{8,9},{9,8},{10,11... | collective-permute-start | bytes 589832 | tf_op jit(solution)/shard_map/ppermute | solution.py:417
  368.2 7.6 %collective-permute-start.20 = (bf16[64,1536]{1,0:T(8,128)(2,1)S(1)}, bf16[64,1536]{1,0:T(8,128)(2,1)S(1)}, u32[]{:S(2)}, u32[]{:S(2)}) collective-permute-start(bf16[64,1536]{1,0:T(8,128)(2,1)S(1)} %get-tuple-element.64), channel_id=1, source_target_pairs={{0,1},{1,0},{2,3},{3,2},{4,5},{5,4},{6,7},{7,6},{8,9},{9,8},{10,11... | collective-permute-start | bytes 589832 | tf_op jit(solution)/shard_map/ppermute | solution.py:417
Sparse Core Ops, SparseCore 0:
  9.1 45.8 all-gather.4
  56.8 93.2 all-gather.6

commit v2 on v1

--- a/solution.py
+++ b/solution.py
@@ -183,7 +183,7 @@
             bytes_accessed=(1 if first else 12) * 2**20,
             transcendentals=0 if first else heads * rows * total,
         ),
-        compiler_params=pltpu.CompilerParams(vmem_limit_bytes=60 * 2**20),
+        compiler_params=pltpu.CompilerParams(vmem_limit_bytes=58 * 2**20),
     )(*args)
 
 
@@ -287,11 +287,10 @@
     other[...] = product[pl.ds(pl.multiple_of((1 - xh) * rows, rows), rows), :].astype(bf16)
 
 
-def project(mixed, weight, part, parts):
-    tokens, width = mixed.shape[1] // 2, weight.shape[2] // parts
+def project(mixed, weight):
+    tokens, width = mixed.shape[1] // 2, weight.shape[2]
     tile = 512
-    start = part * width // tile
-    columns = pl.BlockSpec(weight.shape[:2] + (tile,), lambda n: (0, 0, start + n))
+    columns = pl.BlockSpec(weight.shape[:2] + (tile,), lambda n: (0, 0, n))
     out = pl.BlockSpec((tokens, tile), lambda n: (0, n))
     return pl.pallas_call(
         project_kernel,
@@ -352,8 +351,9 @@
     key_subject = jnp.arange(SUBJ * IDTOK, dtype=jnp.int32) // IDTOK
     match = ((key_subject[None, :] == subject[:, None]) & has_id[:, None]).astype(f32)
     flat_weight = id_kv_weight.reshape(width, 2 * here)
-    got, match, flat_weight, out_weight = lax.optimization_barrier((got, match, flat_weight, out_weight))
-    weight = lax.all_gather(out_weight, "y", axis=0)
+    half_weight = jnp.where(my_c == 0, out_weight[:, : width // 2], out_weight[:, width // 2 :])
+    got, match, flat_weight, half_weight = lax.optimization_barrier((got, match, flat_weight, half_weight))
+    weight = lax.all_gather(half_weight, "y", axis=0)
     q_own, kv = lax.optimization_barrier((got[:, :here], got[:, here:]))
     q_x = lax.ppermute(q_own, "xl", SWAP)
     queries = [q_own, q_x, lax.ppermute(q_own, "c", SWAP), lax.ppermute(q_x, "c", SWAP)]
@@ -406,16 +406,23 @@
     lr_core = lax.ppermute(lr_send, "c", SWAP)
     lr_x = lax.ppermute(lr_keep, "xl", SWAP)
     lr_far = lax.ppermute(lr_send, ("xl", "c"), [(i, 3 - i) for i in range(4)])
+    weight, recv, lr_core, lr_x, lr_far, idpart = lax.optimization_barrier(
+        (weight, recv, lr_core, lr_x, lr_far, idpart)
+    )
+    other_weight = lax.ppermute(weight, "c", SWAP)
     mixed = combine(keep, recv, lr_keep, lr_core, lr_x, lr_far, idpart)
 
     quarter = tok_blk // y_size
     mixed = mixed.reshape(2 * y_size, quarter, here)
+    weight, mixed = lax.optimization_barrier((weight, mixed))
     mixed = lax.all_to_all(mixed, ("xl", "y"), 0, 0, tiled=True)
     out = []
-    for part in range(2):
-        mine, other = project(mixed, weight, part, 2)
+    for columns in (weight, other_weight):
+        mine, other = project(mixed, columns)
         out.append((mine + lax.ppermute(other, "xh", SWAP).astype(f32)).astype(bf16))
-    return jnp.concatenate(out, axis=1)
+    low = jnp.where(my_c == 0, out[0], out[1])
+    high = jnp.where(my_c == 0, out[1], out[0])
+    return jnp.concatenate([low, high], axis=1)
 
 
 def solution(mesh):

time: 386 us -> 383 us (level)
  local copies, waits for them, and re-layouts: 17.1 us -> 11.6 us
    unnamed x38 -> x40, local copies, waits for them, and re-layouts: 14.3 us -> 9.77 us
  transfers between devices with their start and end apart: 24 -> 25, of which waited for: 9 -> 9; matrix products, arithmetic and copies ran while one was open for 5% -> 5% of each run, Pallas kernels for 67% -> 68%
where the time goes in v2:
time: 383 us; the launch traced here: 381 us
  Pallas kernels  259 us (68%)
  starting transfers between devices  33 us (9%)
  waiting for transfers between devices  31.5 us (8%)
  blocking collectives  17.8 us (5%)
  between operations  14.5 us (4%)
  local copies, waits for them, and re-layouts  11.6 us (3%)
  other arithmetic  8.37 us (2%)
  matrix products  5.17 us (1%)
    pallas_call x5, Pallas kernels, attend(): pl.pallas_call(functools.partial(attn_kernel, pieces, marks, marks_all, f...  253 us
    all_to_all x1, blocking collectives, on_device(): mixed = lax.all_to_all(mixed, ('xl', 'y'), 0, 0, tiled=True)  17.8 us
    ppermute x6, waiting for transfers between devices, on_device(): up, down = (lax.ppermute(up, 'z', right), lax.ppermute(down, 'z', left))  12.7 us
    ppermute x6, starting transfers between devices, on_device(): up, down = (lax.ppermute(up, 'z', right), lax.ppermute(down, 'z', left))  12.4 us
    unnamed x40, local copies, waits for them, and re-layouts  9.77 us
  transfers between devices with their start and end apart: 25, of which 9 were waited for; matrix products, arithmetic and copies ran while one was open for 5% of the time, Pallas kernels for 68%

profile of v2, /device:TPU:6, one launch (start us, length us, event | category | flops | bytes accessed | tf_op | source)
XLA Modules:
  0.0 380.7 jit_solution(13198719003638256271)
XLA Ops:
  6.6 0.7 tile.8
  7.3 1.6 pad_maximum_fusion.1
  9.6 1.5 copy.26
  11.5 1.2 maximum_bitcast_fusion
  12.8 7.6 %all-to-all-start = ((bf16[8,64,1152]{2,1,0:T(8,128)(2,1)}), bf16[8,64,1152]{2,1,0:T(8,128)(2,1)S(1)}, u32[]{:S(2)}, u32[]{:S(2)}) async-start(bf16[8,64,1152]{2,1,0:T(8,128)(2,1)} %maximum_bitcast_fusion), calls=%async_computation | async-start | bytes 2359296 | tf_op jit(solution)/shard_map/all_to_all | solution.py:344
  20.4 0.7 fusion.10
  21.0 5.5 %copy.27 = bf16[384,8,2,384]{3,1,2,0:T(8,128)(2,1)} copy(bf16[384,8,2,384]{3,2,1,0:T(2,128)(2,1)} %bitcast.65) | data formatting | bytes 9437184
  26.5 2.5 select_add_fusion
  29.3 1.2 slice_select_fusion
  30.5 5.8 %all-to-all-done = bf16[8,64,1152]{2,1,0:T(8,128)(2,1)S(1)} async-done(((bf16[8,64,1152]{2,1,0:T(8,128)(2,1)}), bf16[8,64,1152]{2,1,0:T(8,128)(2,1)S(1)}, u32[]{:S(2)}, u32[]{:S(2)}) %all-to-all-start) | async-done | bytes 1179680 | tf_op jit(solution)/shard_map/all_to_all | solution.py:344
  36.4 0.9 collective-permute-start
  37.3 1.9 collective-permute-start.3
  39.2 3.9 %collective-permute-start.4 = (bf16[512,768]{1,0:T(8,128)(2,1)S(1)}, bf16[512,768]{1,0:T(8,128)(2,1)}, u32[]{:S(2)}, u32[]{:S(2)}) collective-permute-start(bf16[512,768]{1,0:T(8,128)(2,1)S(1)} %slice.71.refs_5_.refs_6_.refs_10_), channel_id=1, source_target_pairs={{0,112},{16,0},{32,16},{48,32},{64,48},{80,64},{96,80},{112,96},{1... | collective-permute-start | bytes 2359304 | tf_op jit(solution)/shard_map/ppermute | solution.py:371
  43.2 3.0 collective-permute-done.refs_2_
  46.2 1.7 collective-permute-done.2.refs_4_
  47.9 0.8 copy-done.9
  48.7 7.4 %shard_map.100.refs_9_ = f32[3,2048,256]{2,1,0:T(8,128)} custom-call(s32[1]{0:T(128)} %copy.33.refs_0_, bf16[512,384]{1,0:T(8,128)(2,1)} %copy-done, bf16[512,384]{1,0:T(8,128)(2,1)} %copy-done.7, bf16[512,384]{1,0:T(8,128)(2,1)} %copy-done.8, bf16[512,384]{1,0:T(8,128)(2,1)} %copy-done.9, bf16[512,768]{1,0:T(8,128)(2,1)} %copy-done.5, ...), custom_call_target="tpu_custom_call" | custom-call | flops 3145728 | bytes 1048576 | tf_op jit(solution)/shard_map/pallas_call | solution.py:174
  56.1 8.2 %collective-permute-done.3.refs_5_.refs_7_.refs_11_ = bf16[512,768]{1,0:T(8,128)(2,1)} collective-permute-done((bf16[512,768]{1,0:T(8,128)(2,1)S(1)}, bf16[512,768]{1,0:T(8,128)(2,1)}, u32[]{:S(2)}, u32[]{:S(2)}) %collective-permute-start.3) | collective-permute-done | bytes 786464 | tf_op jit(solution)/shard_map/ppermute | solution.py:371
  64.7 2.8 collective-permute-start.6
  67.5 11.6 %shard_map.101.refs_9_ = f32[3,2048,256]{2,1,0:T(8,128)} custom-call(s32[1]{0:T(128)} %copy.33.refs_0_, bf16[512,384]{1,0:T(8,128)(2,1)} %copy-done, bf16[512,384]{1,0:T(8,128)(2,1)} %copy-done.7, bf16[512,384]{1,0:T(8,128)(2,1)} %copy-done.8, bf16[512,384]{1,0:T(8,128)(2,1)} %copy-done.9, bf16[512,768]{1,0:T(8,128)(2,1)} %collective-permute-done.3.refs_5_.refs_7_.refs_11_, ...), custom_call_target="tpu_custom_call" | custom-call | flops 12884901888 | bytes 12582912 | tf_op jit(solution)/shard_map/pallas_call | solution.py:174
  79.1 1.9 fusion
  81.2 3.3 collective-permute-done.5.refs_5_.refs_7_.refs_13_
  84.5 1.0 collective-permute-start.7
  85.5 2.3 collective-permute-start.8
  88.0 1.2 collective-permute-start.10
  89.2 11.4 %shard_map.102.refs_9_ = f32[3,2048,256]{2,1,0:T(8,128)} custom-call(s32[1]{0:T(128)} %copy.33.refs_0_, bf16[512,384]{1,0:T(8,128)(2,1)} %copy-done, bf16[512,384]{1,0:T(8,128)(2,1)} %copy-done.7, bf16[512,384]{1,0:T(8,128)(2,1)} %copy-done.8, bf16[512,384]{1,0:T(8,128)(2,1)} %copy-done.9, bf16[512,768]{1,0:T(8,128)(2,1)} %collective-permute-done.5.refs_5_.refs_7_.refs_13_, ...), custom_call_target="tpu_custom_call" | custom-call | flops 12884901888 | bytes 12582912 | tf_op jit(solution)/shard_map/pallas_call | solution.py:174
  101.3 3.3 convolution_convert_fusion
  104.6 1.3 collective-permute-done.7.refs_5_.refs_7_.refs_15_
  106.0 1.0 collective-permute-start.11
  107.0 2.6 collective-permute-start.12
  109.7 11.3 %shard_map.103.refs_9_ = f32[3,2048,256]{2,1,0:T(8,128)} custom-call(s32[1]{0:T(128)} %copy.33.refs_0_, bf16[512,384]{1,0:T(8,128)(2,1)} %copy-done, bf16[512,384]{1,0:T(8,128)(2,1)} %copy-done.7, bf16[512,384]{1,0:T(8,128)(2,1)} %copy-done.8, bf16[512,384]{1,0:T(8,128)(2,1)} %copy-done.9, bf16[512,768]{1,0:T(8,128)(2,1)} %copy-done.11, ...), custom_call_target="tpu_custom_call" | custom-call | flops 12884901888 | bytes 12582912 | tf_op jit(solution)/shard_map/pallas_call | solution.py:174
  121.0 0.7 copy-done.17
  121.8 0.7 copy-done.18
  122.5 211.2 %shard_map.104 = (bf16[1024,384]{1,0:T(8,128)(2,1)}, bf16[1024,384]{1,0:T(8,128)(2,1)}, f32[3,2,1024]{2,1,0:T(2,128)}, f32[3,2,1024]{2,1,0:T(2,128)}) custom-call(s32[1]{0:T(128)} %copy.33.refs_0_, bf16[512,384]{1,0:T(8,128)(2,1)} %copy-done, bf16[512,384]{1,0:T(8,128)(2,1)} %copy-done.7, bf16[512,384]{1,0:T(8,128)(2,1)} %copy-done.8, ...), custom_call_target="tpu_custom_call" | custom-call | flops 6442450944 | bytes 12582912 | tf_op jit(solution)/shard_map/pallas_call | solution.py:174
  333.9 1.2 collective-permute-start.18
  335.2 0.9 collective-permute-start.17
  336.1 1.1 collective-permute-start.16
  337.2 2.3 collective-permute-done.18
  339.6 0.8 shard_map.105.id_ref
  340.6 1.3 shard_map.106
  341.9 17.8 %all_to_all.10.mixed = bf16[8,128,384]{2,1,0:T(8,128)(2,1)S(1)} all-to-all(bf16[8,128,384]{2,1,0:T(8,128)(2,1)S(1)} %bitcast.59), channel_id=1, replica_groups=mesh['xl'=2,'z'=8,'c'=2,'y'=4,'xh'=2] {'xl','y'}, dimensions={0} | all-to-all | bytes 1572864 | tf_op jit(solution)/shard_map/all_to_all | solution.py:418
  359.7 1.9 shard_map.107
  361.6 1.1 collective-permute-start.19
  362.7 1.9 shard_map.108
  364.6 2.6 collective-permute-start.21
  367.2 3.3 collective-permute-done.19
  370.5 2.6 collective-permute-done.21
  373.1 0.8 pad_maximum_fusion
  (85 shorter events, 3.0 us)
Async XLA Ops:
  6.5 72.6 %all-gather.7.cloned.1.call-start = ((), (), s32[]{:S(2)}) async-start(), calls=%async_computation.3 | async-start | bytes 1843200 | tf_op jit(solution)/shard_map/all_gather | solution.py:337
  12.8 7.6 %copy-start.14 = (s32[512]{0:T(512)S(1)}, s32[512]{0:T(512)}, u32[]{:S(2)}) copy-start(s32[512]{0:T(512)} %param.12) | copy-start | bytes 6148
  12.8 7.6 %copy-start.15 = (s32[4]{0:T(128)S(1)}, s32[4]{0:T(128)}, u32[]{:S(2)}) copy-start(s32[4]{0:T(128)} %param.13) | copy-start | bytes 52
  12.8 23.5 %all-to-all-start = ((bf16[8,64,1152]{2,1,0:T(8,128)(2,1)}), bf16[8,64,1152]{2,1,0:T(8,128)(2,1)S(1)}, u32[]{:S(2)}, u32[]{:S(2)}) async-start(bf16[8,64,1152]{2,1,0:T(8,128)(2,1)} %maximum_bitcast_fusion), calls=%async_computation | async-start | bytes 2359296 | tf_op jit(solution)/shard_map/all_to_all | solution.py:344
  20.3 320.1 %all-gather.5.cloned.1.call-start = ((), (), s32[]{:S(2)}) async-start(), calls=%async_computation.2 | async-start | bytes 5898240 | tf_op jit(solution)/shard_map/all_gather | solution.py:356
  21.0 8.2 %copy-start.6 = (bf16[384,3072]{1,0:T(8,128)(2,1)S(1)}, bf16[384,3072]{1,0:T(8,128)(2,1)}, u32[]{:S(2)}) copy-start(bf16[384,3072]{1,0:T(8,128)(2,1)} %param.19) | copy-start | bytes 7077892
  36.3 11.6 %copy-start.5 = (bf16[512,768]{1,0:T(8,128)(2,1)}, bf16[512,768]{1,0:T(8,128)(2,1)S(1)}, u32[]{:S(2)}) copy-start(bf16[512,768]{1,0:T(8,128)(2,1)S(1)} %slice.71.refs_5_.refs_6_.refs_10_) | copy-start | bytes 2359300
  36.4 11.5 %copy-start = (bf16[512,384]{1,0:T(8,128)(2,1)}, bf16[512,384]{1,0:T(8,128)(2,1)S(1)}, u32[]{:S(2)}) copy-start(bf16[512,384]{1,0:T(8,128)(2,1)S(1)} %slice.70.refs_1_.q_ref) | copy-start | bytes 1179652
  36.4 9.8 %collective-permute-start = (bf16[512,384]{1,0:T(8,128)(2,1)S(1)}, bf16[512,384]{1,0:T(8,128)(2,1)S(1)}, u32[]{:S(2)}, u32[]{:S(2)}) collective-permute-start(bf16[512,384]{1,0:T(8,128)(2,1)S(1)} %slice.70.refs_1_.q_ref), channel_id=1, source_target_pairs={{0,128},{128,0},{1,129},{129,1},{2,130},{130,2},{3,131},{131,3},{4... | collective-permute-start | bytes 1179656 | tf_op jit(solution)/shard_map/ppermute | solution.py:358
  37.3 27.0 %collective-permute-start.3 = (bf16[512,768]{1,0:T(8,128)(2,1)S(1)}, bf16[512,768]{1,0:T(8,128)(2,1)}, u32[]{:S(2)}, u32[]{:S(2)}) collective-permute-start(bf16[512,768]{1,0:T(8,128)(2,1)S(1)} %slice.71.refs_5_.refs_6_.refs_10_), channel_id=1, source_target_pairs={{0,16},{16,32},{32,48},{48,64},{64,80},{80,96},{96,112},{112,0},{1... | collective-permute-start | bytes 2359304 | tf_op jit(solution)/shard_map/ppermute | solution.py:371
  39.2 25.1 %collective-permute-start.4 = (bf16[512,768]{1,0:T(8,128)(2,1)S(1)}, bf16[512,768]{1,0:T(8,128)(2,1)}, u32[]{:S(2)}, u32[]{:S(2)}) collective-permute-start(bf16[512,768]{1,0:T(8,128)(2,1)S(1)} %slice.71.refs_5_.refs_6_.refs_10_), channel_id=1, source_target_pairs={{0,112},{16,0},{32,16},{48,32},{64,48},{80,64},{96,80},{112,96},{1... | collective-permute-start | bytes 2359304 | tf_op jit(solution)/shard_map/ppermute | solution.py:371
  43.2 3.0 collective-permute-start.1
  46.2 1.7 copy-start.7
  46.2 1.7 collective-permute-start.2
  46.2 1.7 copy-start.8
  47.9 0.8 copy-start.9
  64.3 20.2 %collective-permute-start.5 = (bf16[512,768]{1,0:T(8,128)(2,1)}, bf16[512,768]{1,0:T(8,128)(2,1)}, u32[]{:S(2)}, u32[]{:S(2)}) collective-permute-start(bf16[512,768]{1,0:T(8,128)(2,1)} %collective-permute-done.3.refs_5_.refs_7_.refs_11_), channel_id=1, source_target_pairs={{0,16},{16,32},{32,48},{48,64},{64,80},{80,96},{96,112},{112,0},{1... | collective-permute-start | bytes 2359304 | tf_op jit(solution)/shard_map/ppermute | solution.py:371
  64.7 19.8 %collective-permute-start.6 = (bf16[512,768]{1,0:T(8,128)(2,1)}, bf16[512,768]{1,0:T(8,128)(2,1)S(1)}, u32[]{:S(2)}, u32[]{:S(2)}) collective-permute-start(bf16[512,768]{1,0:T(8,128)(2,1)} %collective-permute-done.4.refs_6_.refs_8_.refs_12_), channel_id=1, source_target_pairs={{0,112},{16,0},{32,16},{48,32},{64,48},{80,64},{96,80},{112,96},{1... | collective-permute-start | bytes 2359304 | tf_op jit(solution)/shard_map/ppermute | solution.py:371
  84.5 4.7 %copy-start.16 = (bf16[512,768]{1,0:T(8,128)(2,1)}, bf16[512,768]{1,0:T(8,128)(2,1)S(1)}, u32[]{:S(2)}) copy-start(bf16[512,768]{1,0:T(8,128)(2,1)S(1)} %collective-permute-done.6.refs_6_.refs_8_.refs_14_) | copy-start | bytes 2359300
  84.5 3.3 collective-permute-start.9
  84.5 21.4 %collective-permute-start.7 = (bf16[512,768]{1,0:T(8,128)(2,1)}, bf16[512,768]{1,0:T(8,128)(2,1)S(1)}, u32[]{:S(2)}, u32[]{:S(2)}) collective-permute-start(bf16[512,768]{1,0:T(8,128)(2,1)} %collective-permute-done.5.refs_5_.refs_7_.refs_13_), channel_id=1, source_target_pairs={{0,16},{16,32},{32,48},{48,64},{64,80},{80,96},{96,112},{112,0},{1... | collective-permute-start | bytes 2359304 | tf_op jit(solution)/shard_map/ppermute | solution.py:371
  85.5 20.4 %collective-permute-start.8 = (bf16[512,768]{1,0:T(8,128)(2,1)S(1)}, bf16[512,768]{1,0:T(8,128)(2,1)S(1)}, u32[]{:S(2)}, u32[]{:S(2)}) collective-permute-start(bf16[512,768]{1,0:T(8,128)(2,1)S(1)} %collective-permute-done.6.refs_6_.refs_8_.refs_14_), channel_id=1, source_target_pairs={{0,112},{16,0},{32,16},{48,32},{64,48},{80,64},{96,80},{112,96},{1... | collective-permute-start | bytes 2359304 | tf_op jit(solution)/shard_map/ppermute | solution.py:371
  88.0 12.7 %copy-start.10 = (bf16[32,3072]{1,0:T(8,128)(2,1)S(1)}, bf16[32,3072]{1,0:T(8,128)(2,1)}, u32[]{:S(2)}) copy-start(bf16[32,3072]{1,0:T(8,128)(2,1)} %param.16) | copy-start | bytes 589828
  88.0 12.7 %collective-permute-start.10 = (f32[32,3072]{1,0:T(8,128)S(1)}, f32[32,3072]{1,0:T(8,128)S(1)}, u32[]{:S(2)}, u32[]{:S(2)}) collective-permute-start(f32[32,3072]{1,0:T(8,128)S(1)} %select_bitcast_fusion.2), channel_id=1, source_target_pairs={{0,128},{128,0},{1,129},{129,1},{2,130},{130,2},{3,131},{131,3},{4... | collective-permute-start | bytes 1179656 | tf_op jit(solution)/shard_map/ppermute | solution.py:387
  100.6 0.7 copy-start.13
  105.9 3.8 copy-start.11
  105.9 3.8 copy-start.12
  105.9 15.1 %collective-permute-start.13 = (bf16[32,768]{1,0:T(8,128)(2,1)S(1)}, bf16[32,768]{1,0:T(8,128)(2,1)S(1)}, u32[]{:S(2)}, u32[]{:S(2)}) collective-permute-start(bf16[32,768]{1,0:T(8,128)(2,1)S(1)} %convolution_convert_fusion), channel_id=1, source_target_pairs={{0,8},{8,0},{1,9},{9,1},{2,10},{10,2},{3,11},{11,3},{4,12},{12,4},... | collective-permute-start | bytes 147464 | tf_op jit(solution)/shard_map/ppermute | solution.py:396
  106.0 15.0 %collective-permute-start.11 = (bf16[256,768]{1,0:T(8,128)(2,1)S(1)}, bf16[256,768]{1,0:T(8,128)(2,1)S(1)}, u32[]{:S(2)}, u32[]{:S(2)}) collective-permute-start(bf16[256,768]{1,0:T(8,128)(2,1)S(1)} %slice.78), channel_id=1, source_target_pairs={{0,16},{16,32},{32,48},{48,64},{64,80},{80,96},{96,112},{112,0},{1... | collective-permute-start | bytes 1179656 | tf_op jit(solution)/shard_map/ppermute | solution.py:374
  107.0 14.0 %collective-permute-start.12 = (bf16[256,768]{1,0:T(8,128)(2,1)S(1)}, bf16[256,768]{1,0:T(8,128)(2,1)S(1)}, u32[]{:S(2)}, u32[]{:S(2)}) collective-permute-start(bf16[256,768]{1,0:T(8,128)(2,1)S(1)} %slice.79), channel_id=1, source_target_pairs={{0,112},{16,0},{32,16},{48,32},{64,48},{80,64},{96,80},{112,96},{1... | collective-permute-start | bytes 1179656 | tf_op jit(solution)/shard_map/ppermute | solution.py:374
  121.0 218.6 %copy-start.1 = (bf16[512,384]{1,0:T(8,128)(2,1)S(1)}, bf16[512,384]{1,0:T(8,128)(2,1)}, u32[]{:S(2)}) copy-start(bf16[512,384]{1,0:T(8,128)(2,1)} %copy-done) | copy-start | bytes 1179652
  121.0 0.8 copy-start.17
  121.8 0.7 copy-start.18
  333.8 6.8 %copy-start.2 = (bf16[1024,384]{1,0:T(8,128)(2,1)S(1)}, bf16[1024,384]{1,0:T(8,128)(2,1)}, u32[]{:S(2)}) copy-start(bf16[1024,384]{1,0:T(8,128)(2,1)} %get-tuple-element.69.keep) | copy-start | bytes 2359300
  333.8 6.8 %copy-start.3 = (f32[3,2,1024]{2,1,0:T(2,128)S(1)}, f32[3,2,1024]{2,1,0:T(2,128)}, u32[]{:S(2)}) copy-start(f32[3,2,1024]{2,1,0:T(2,128)} %get-tuple-element.65.lr_own) | copy-start | bytes 73732
  333.8 6.6 %collective-permute-start.14 = (bf16[1024,384]{1,0:T(8,128)(2,1)}, bf16[1024,384]{1,0:T(8,128)(2,1)S(1)}, u32[]{:S(2)}, u32[]{:S(2)}) collective-permute-start(bf16[1024,384]{1,0:T(8,128)(2,1)} %get-tuple-element.63), channel_id=1, source_target_pairs={{0,8},{8,0},{1,9},{9,1},{2,10},{10,2},{3,11},{11,3},{4,12},{12,4},... | collective-permute-start | bytes 2359304 | tf_op jit(solution)/shard_map/ppermute | solution.py:405
  333.9 5.7 %collective-permute-start.18 = (bf16[2,32,768]{2,1,0:T(8,128)(2,1)S(1)}, bf16[2,32,768]{2,1,0:T(8,128)(2,1)S(1)}, u32[]{:S(2)}, u32[]{:S(2)}) collective-permute-start(bf16[2,32,768]{2,1,0:T(8,128)(2,1)S(1)} %maximum_select_fusion.1), channel_id=1, source_target_pairs={{0,128},{128,0},{1,129},{129,1},{2,130},{130,2},{3,131},{131,3},{4... | collective-permute-start | bytes 294920 | tf_op jit(solution)/shard_map/ppermute | solution.py:399
  335.1 5.3 %collective-permute-start.15 = (f32[3,2,1024]{2,1,0:T(2,128)}, f32[3,2,1024]{2,1,0:T(2,128)S(1)}, u32[]{:S(2)}, u32[]{:S(2)}) collective-permute-start(f32[3,2,1024]{2,1,0:T(2,128)} %get-tuple-element.64), channel_id=1, source_target_pairs={{0,8},{8,0},{1,9},{9,1},{2,10},{10,2},{3,11},{11,3},{4,12},{12,4},... | collective-permute-start | bytes 73736 | tf_op jit(solution)/shard_map/ppermute | solution.py:406
  335.2 5.2 %collective-permute-start.17 = (f32[3,2,1024]{2,1,0:T(2,128)}, f32[3,2,1024]{2,1,0:T(2,128)S(1)}, u32[]{:S(2)}, u32[]{:S(2)}) collective-permute-start(f32[3,2,1024]{2,1,0:T(2,128)} %get-tuple-element.64), channel_id=1, source_target_pairs={{0,136},{8,128},{128,8},{136,0},{1,137},{9,129},{129,9},{137,1},{2... | collective-permute-start | bytes 73736 | tf_op jit(solution)/shard_map/ppermute | solution.py:408
  336.1 4.3 %collective-permute-start.16 = (f32[3,2,1024]{2,1,0:T(2,128)}, f32[3,2,1024]{2,1,0:T(2,128)S(1)}, u32[]{:S(2)}, u32[]{:S(2)}) collective-permute-start(f32[3,2,1024]{2,1,0:T(2,128)} %get-tuple-element.65.lr_own), channel_id=1, source_target_pairs={{0,128},{128,0},{1,129},{129,1},{2,130},{130,2},{3,131},{131,3},{4... | collective-permute-start | bytes 73736 | tf_op jit(solution)/shard_map/ppermute | solution.py:407
  340.5 22.2 %collective-permute-start.20 = (bf16[4,384,1536]{2,1,0:T(8,128)(2,1)}, bf16[4,384,1536]{2,1,0:T(8,128)(2,1)S(1)}, u32[]{:S(2)}, u32[]{:S(2)}) collective-permute-start(bf16[4,384,1536]{2,1,0:T(8,128)(2,1)} %bitcast.61), channel_id=1, source_target_pairs={{0,8},{8,0},{1,9},{9,1},{2,10},{10,2},{3,11},{11,3},{4,12},{12,4},... | collective-permute-start | bytes 14155784 | tf_op jit(solution)/shard_map/ppermute | solution.py:412
  340.6 19.1 %copy-start.4 = (bf16[1536,1536]{1,0:T(8,128)(2,1)S(1)}, bf16[1536,1536]{1,0:T(8,128)(2,1)}, u32[]{:S(2)}) copy-start(bf16[1536,1536]{1,0:T(8,128)(2,1)} %all-gather.5.cloned.1.call-done) | copy-start | bytes 14155780
  361.6 8.9 %collective-permute-start.19 = (bf16[64,1536]{1,0:T(8,128)(2,1)S(1)}, bf16[64,1536]{1,0:T(8,128)(2,1)S(1)}, u32[]{:S(2)}, u32[]{:S(2)}) collective-permute-start(bf16[64,1536]{1,0:T(8,128)(2,1)S(1)} %get-tuple-element.78), channel_id=1, source_target_pairs={{0,1},{1,0},{2,3},{3,2},{4,5},{5,4},{6,7},{7,6},{8,9},{9,8},{10,11... | collective-permute-start | bytes 589832 | tf_op jit(solution)/shard_map/ppermute | solution.py:422
  364.6 8.5 %collective-permute-start.21 = (bf16[64,1536]{1,0:T(8,128)(2,1)S(1)}, bf16[64,1536]{1,0:T(8,128)(2,1)S(1)}, u32[]{:S(2)}, u32[]{:S(2)}) collective-permute-start(bf16[64,1536]{1,0:T(8,128)(2,1)S(1)} %get-tuple-element.80), channel_id=1, source_target_pairs={{0,1},{1,0},{2,3},{3,2},{4,5},{5,4},{6,7},{7,6},{8,9},{9,8},{10,11... | collective-permute-start | bytes 589832 | tf_op jit(solution)/shard_map/ppermute | solution.py:422
Sparse Core Ops, SparseCore 0:
  9.1 45.7 all-gather.6
  56.8 53.8 all-gather.4

commit v3 on v2

--- a/solution.py
+++ b/solution.py
@@ -183,7 +183,7 @@
             bytes_accessed=(1 if first else 12) * 2**20,
             transcendentals=0 if first else heads * rows * total,
         ),
-        compiler_params=pltpu.CompilerParams(vmem_limit_bytes=58 * 2**20),
+        compiler_params=pltpu.CompilerParams(vmem_limit_bytes=(50 if last else 58) * 2**20),
     )(*args)
 
 

time: 383 us -> 372 us (0.971)
  Pallas kernels: 259 us -> 248 us
    pallas_call x5, Pallas kernels: 253 us -> 242 us  [attend(): pl.pallas_call(functools.partial(attn_kernel, pieces, marks, marks_all, f...]
    unnamed x40 -> x38, local copies, waits for them, and re-layouts: 9.77 us -> 9.16 us
  transfers between devices with their start and end apart: 25 -> 25, of which waited for: 9 -> 9; matrix products, arithmetic and copies ran while one was open for 5% -> 5% of each run, Pallas kernels for 68% -> 67%
where the time goes in v3:
time: 372 us; the launch traced here: 370 us
  Pallas kernels  248 us (67%)
  starting transfers between devices  32.8 us (9%)
  waiting for transfers between devices  31.3 us (8%)
  blocking collectives  17.8 us (5%)
  between operations  14.5 us (4%)
  local copies, waits for them, and re-layouts  12 us (3%)
  other arithmetic  8.4 us (2%)
  matrix products  5.17 us (1%)
    pallas_call x5, Pallas kernels, attend(): pl.pallas_call(functools.partial(attn_kernel, pieces, marks, marks_all, f...  242 us
    all_to_all x1, blocking collectives, on_device(): mixed = lax.all_to_all(mixed, ('xl', 'y'), 0, 0, tiled=True)  17.8 us
    ppermute x6, waiting for transfers between devices, on_device(): up, down = (lax.ppermute(up, 'z', right), lax.ppermute(down, 'z', left))  12.5 us
    ppermute x6, starting transfers between devices, on_device(): up, down = (lax.ppermute(up, 'z', right), lax.ppermute(down, 'z', left))  12.3 us
    unnamed x38, local copies, waits for them, and re-layouts  9.16 us
    all_to_all x1, starting transfers between devices, on_device(): got = lax.all_to_all(sent, ULY, 0, 0, tiled=True).reshape(tok_blk, 3 * here)  7.56 us
  transfers between devices with their start and end apart: 25, of which 9 were waited for; matrix products, arithmetic and copies ran while one was open for 5% of the time, Pallas kernels for 67%

profile of v3, /device:TPU:6, one launch (start us, length us, event | category | flops | bytes accessed | tf_op | source)
XLA Modules:
  0.0 370.2 jit_solution(9848306249259798756)
XLA Ops:
  6.6 0.7 tile.8
  7.3 1.6 pad_maximum_fusion.1
  9.7 1.5 copy.26
  11.6 1.2 maximum_bitcast_fusion
  12.8 7.6 %all-to-all-start = ((bf16[8,64,1152]{2,1,0:T(8,128)(2,1)}), bf16[8,64,1152]{2,1,0:T(8,128)(2,1)S(1)}, u32[]{:S(2)}, u32[]{:S(2)}) async-start(bf16[8,64,1152]{2,1,0:T(8,128)(2,1)} %maximum_bitcast_fusion), calls=%async_computation | async-start | bytes 2359296 | tf_op jit(solution)/shard_map/all_to_all | solution.py:344
  20.4 0.7 fusion.10
  21.1 5.5 %copy.27 = bf16[384,8,2,384]{3,1,2,0:T(8,128)(2,1)} copy(bf16[384,8,2,384]{3,2,1,0:T(2,128)(2,1)} %bitcast.65) | data formatting | bytes 9437184
  26.5 2.5 select_add_fusion
  29.3 1.2 slice_select_fusion
  30.5 5.8 %all-to-all-done = bf16[8,64,1152]{2,1,0:T(8,128)(2,1)S(1)} async-done(((bf16[8,64,1152]{2,1,0:T(8,128)(2,1)}), bf16[8,64,1152]{2,1,0:T(8,128)(2,1)S(1)}, u32[]{:S(2)}, u32[]{:S(2)}) %all-to-all-start) | async-done | bytes 1179680 | tf_op jit(solution)/shard_map/all_to_all | solution.py:344
  36.4 0.9 collective-permute-start
  37.3 1.9 collective-permute-start.3
  39.3 3.9 %collective-permute-start.4 = (bf16[512,768]{1,0:T(8,128)(2,1)S(1)}, bf16[512,768]{1,0:T(8,128)(2,1)}, u32[]{:S(2)}, u32[]{:S(2)}) collective-permute-start(bf16[512,768]{1,0:T(8,128)(2,1)S(1)} %slice.71.refs_5_.refs_6_.refs_10_), channel_id=1, source_target_pairs={{0,112},{16,0},{32,16},{48,32},{64,48},{80,64},{96,80},{112,96},{1... | collective-permute-start | bytes 2359304 | tf_op jit(solution)/shard_map/ppermute | solution.py:371
  43.2 3.0 collective-permute-done.refs_2_
  46.2 1.7 collective-permute-done.2.refs_4_
  47.9 0.8 copy-done.6
  48.7 7.4 %shard_map.100.refs_9_ = f32[3,2048,256]{2,1,0:T(8,128)} custom-call(s32[1]{0:T(128)} %copy.33.refs_0_, bf16[512,384]{1,0:T(8,128)(2,1)} %copy-done, bf16[512,384]{1,0:T(8,128)(2,1)} %copy-done.2, bf16[512,384]{1,0:T(8,128)(2,1)} %copy-done.4, bf16[512,384]{1,0:T(8,128)(2,1)} %copy-done.6, bf16[512,768]{1,0:T(8,128)(2,1)} %copy-done.9, ...), custom_call_target="tpu_custom_call" | custom-call | flops 3145728 | bytes 1048576 | tf_op jit(solution)/shard_map/pallas_call | solution.py:174
  56.1 8.1 %collective-permute-done.3.refs_5_.refs_7_.refs_11_ = bf16[512,768]{1,0:T(8,128)(2,1)S(1)} collective-permute-done((bf16[512,768]{1,0:T(8,128)(2,1)S(1)}, bf16[512,768]{1,0:T(8,128)(2,1)S(1)}, u32[]{:S(2)}, u32[]{:S(2)}) %collective-permute-start.3) | collective-permute-done | bytes 786464 | tf_op jit(solution)/shard_map/ppermute | solution.py:371
  64.7 2.7 collective-permute-start.6
  67.4 11.6 %shard_map.101.refs_9_ = f32[3,2048,256]{2,1,0:T(8,128)} custom-call(s32[1]{0:T(128)} %copy.33.refs_0_, bf16[512,384]{1,0:T(8,128)(2,1)} %copy-done, bf16[512,384]{1,0:T(8,128)(2,1)} %copy-done.2, bf16[512,384]{1,0:T(8,128)(2,1)} %copy-done.4, bf16[512,384]{1,0:T(8,128)(2,1)} %copy-done.6, bf16[512,768]{1,0:T(8,128)(2,1)} %copy-done.16, ...), custom_call_target="tpu_custom_call" | custom-call | flops 12884901888 | bytes 12582912 | tf_op jit(solution)/shard_map/pallas_call | solution.py:174
  79.1 1.9 fusion
  81.1 3.0 collective-permute-done.5.refs_5_.refs_7_.refs_13_
  84.1 0.9 copy-done.17
  85.0 0.6 collective-permute-start.7
  85.6 2.6 collective-permute-start.8
  88.4 1.2 collective-permute-start.10
  89.6 11.4 %shard_map.102.refs_9_ = f32[3,2048,256]{2,1,0:T(8,128)} custom-call(s32[1]{0:T(128)} %copy.33.refs_0_, bf16[512,384]{1,0:T(8,128)(2,1)} %copy-done, bf16[512,384]{1,0:T(8,128)(2,1)} %copy-done.2, bf16[512,384]{1,0:T(8,128)(2,1)} %copy-done.4, bf16[512,384]{1,0:T(8,128)(2,1)} %copy-done.6, bf16[512,768]{1,0:T(8,128)(2,1)} %copy-done.17, ...), custom_call_target="tpu_custom_call" | custom-call | flops 12884901888 | bytes 12582912 | tf_op jit(solution)/shard_map/pallas_call | solution.py:174
  101.7 3.3 convolution_convert_fusion
  105.0 1.4 collective-permute-done.7.refs_5_.refs_7_.refs_15_
  106.4 1.0 collective-permute-start.11
  107.4 1.0 slice.79
  108.5 2.6 collective-permute-start.12
  111.1 11.3 %shard_map.103.refs_9_ = f32[3,2048,256]{2,1,0:T(8,128)} custom-call(s32[1]{0:T(128)} %copy.33.refs_0_, bf16[512,384]{1,0:T(8,128)(2,1)} %copy-done, bf16[512,384]{1,0:T(8,128)(2,1)} %copy-done.2, bf16[512,384]{1,0:T(8,128)(2,1)} %copy-done.4, bf16[512,384]{1,0:T(8,128)(2,1)} %copy-done.6, bf16[512,768]{1,0:T(8,128)(2,1)} %copy-done.12, ...), custom_call_target="tpu_custom_call" | custom-call | flops 12884901888 | bytes 12582912 | tf_op jit(solution)/shard_map/pallas_call | solution.py:174
  122.5 200.7 %shard_map.104 = (bf16[1024,384]{1,0:T(8,128)(2,1)S(1)}, bf16[1024,384]{1,0:T(8,128)(2,1)S(1)}, f32[3,2,1024]{2,1,0:T(2,128)S(1)}, f32[3,2,1024]{2,1,0:T(2,128)S(1)}) custom-call(s32[1]{0:T(128)} %copy.33.refs_0_, bf16[512,384]{1,0:T(8,128)(2,1)S(1)} %copy-done.1, bf16[512,384]{1,0:T(8,128)(2,1)S(1)} %copy-done.3, bf16[512,384]{1,0:T(8,128)(2,1)S(1)} %copy-done.5, ...), custom_call_target="tpu_custom_call" | custom-call | flops 6442450944 | bytes 12582912 | tf_op jit(solution)/shard_map/pallas_call | solution.py:174
  323.3 1.1 collective-permute-start.18
  324.6 0.9 collective-permute-start.17
  325.5 1.1 collective-permute-start.16
  326.6 2.4 collective-permute-done.18
  329.0 0.8 shard_map.105.id_ref
  330.0 1.3 shard_map.106
  331.3 17.8 %all_to_all.10.mixed = bf16[8,128,384]{2,1,0:T(8,128)(2,1)S(1)} all-to-all(bf16[8,128,384]{2,1,0:T(8,128)(2,1)S(1)} %bitcast.59), channel_id=1, replica_groups=mesh['xl'=2,'z'=8,'c'=2,'y'=4,'xh'=2] {'xl','y'}, dimensions={0} | all-to-all | bytes 1572864 | tf_op jit(solution)/shard_map/all_to_all | solution.py:418
  349.1 1.9 shard_map.107
  351.0 1.1 collective-permute-start.19
  352.1 1.9 shard_map.108
  354.0 2.6 collective-permute-start.21
  356.6 3.3 collective-permute-done.19
  359.9 2.5 collective-permute-done.21
  362.5 0.8 pad_maximum_fusion
  (83 shorter events, 3.0 us)
Async XLA Ops:
  6.5 72.5 %all-gather.7.cloned.1.call-start = ((), (), s32[]{:S(2)}) async-start(), calls=%async_computation.3 | async-start | bytes 1843200 | tf_op jit(solution)/shard_map/all_gather | solution.py:337
  12.8 7.6 %copy-start.14 = (s32[512]{0:T(512)S(1)}, s32[512]{0:T(512)}, u32[]{:S(2)}) copy-start(s32[512]{0:T(512)} %param.12) | copy-start | bytes 6148
  12.8 7.6 %copy-start.15 = (s32[4]{0:T(128)S(1)}, s32[4]{0:T(128)}, u32[]{:S(2)}) copy-start(s32[4]{0:T(128)} %param.13) | copy-start | bytes 52
  12.8 23.5 %all-to-all-start = ((bf16[8,64,1152]{2,1,0:T(8,128)(2,1)}), bf16[8,64,1152]{2,1,0:T(8,128)(2,1)S(1)}, u32[]{:S(2)}, u32[]{:S(2)}) async-start(bf16[8,64,1152]{2,1,0:T(8,128)(2,1)} %maximum_bitcast_fusion), calls=%async_computation | async-start | bytes 2359296 | tf_op jit(solution)/shard_map/all_to_all | solution.py:344
  20.4 309.5 %all-gather.5.cloned.1.call-start = ((), (), s32[]{:S(2)}) async-start(), calls=%async_computation.2 | async-start | bytes 5898240 | tf_op jit(solution)/shard_map/all_gather | solution.py:356
  21.1 8.2 %copy-start.10 = (bf16[384,3072]{1,0:T(8,128)(2,1)S(1)}, bf16[384,3072]{1,0:T(8,128)(2,1)}, u32[]{:S(2)}) copy-start(bf16[384,3072]{1,0:T(8,128)(2,1)} %param.19) | copy-start | bytes 7077892
  36.4 11.6 %copy-start.9 = (bf16[512,768]{1,0:T(8,128)(2,1)}, bf16[512,768]{1,0:T(8,128)(2,1)S(1)}, u32[]{:S(2)}) copy-start(bf16[512,768]{1,0:T(8,128)(2,1)S(1)} %slice.71.refs_5_.refs_6_.refs_10_) | copy-start | bytes 2359300
  36.4 11.5 %copy-start = (bf16[512,384]{1,0:T(8,128)(2,1)}, bf16[512,384]{1,0:T(8,128)(2,1)S(1)}, u32[]{:S(2)}) copy-start(bf16[512,384]{1,0:T(8,128)(2,1)S(1)} %slice.70.refs_1_.q_ref) | copy-start | bytes 1179652
  36.4 9.8 %collective-permute-start = (bf16[512,384]{1,0:T(8,128)(2,1)S(1)}, bf16[512,384]{1,0:T(8,128)(2,1)S(1)}, u32[]{:S(2)}, u32[]{:S(2)}) collective-permute-start(bf16[512,384]{1,0:T(8,128)(2,1)S(1)} %slice.70.refs_1_.q_ref), channel_id=1, source_target_pairs={{0,128},{128,0},{1,129},{129,1},{2,130},{130,2},{3,131},{131,3},{4... | collective-permute-start | bytes 1179656 | tf_op jit(solution)/shard_map/ppermute | solution.py:358
  37.3 26.9 %collective-permute-start.3 = (bf16[512,768]{1,0:T(8,128)(2,1)S(1)}, bf16[512,768]{1,0:T(8,128)(2,1)S(1)}, u32[]{:S(2)}, u32[]{:S(2)}) collective-permute-start(bf16[512,768]{1,0:T(8,128)(2,1)S(1)} %slice.71.refs_5_.refs_6_.refs_10_), channel_id=1, source_target_pairs={{0,16},{16,32},{32,48},{48,64},{64,80},{80,96},{96,112},{112,0},{1... | collective-permute-start | bytes 2359304 | tf_op jit(solution)/shard_map/ppermute | solution.py:371
  39.3 24.9 %collective-permute-start.4 = (bf16[512,768]{1,0:T(8,128)(2,1)S(1)}, bf16[512,768]{1,0:T(8,128)(2,1)}, u32[]{:S(2)}, u32[]{:S(2)}) collective-permute-start(bf16[512,768]{1,0:T(8,128)(2,1)S(1)} %slice.71.refs_5_.refs_6_.refs_10_), channel_id=1, source_target_pairs={{0,112},{16,0},{32,16},{48,32},{64,48},{80,64},{96,80},{112,96},{1... | collective-permute-start | bytes 2359304 | tf_op jit(solution)/shard_map/ppermute | solution.py:371
  43.2 3.0 collective-permute-start.1
  46.2 1.7 copy-start.2
  46.2 1.7 collective-permute-start.2
  46.2 1.7 copy-start.4
  47.9 0.8 copy-start.6
  64.2 3.2 copy-start.16
  64.2 19.9 %collective-permute-start.5 = (bf16[512,768]{1,0:T(8,128)(2,1)S(1)}, bf16[512,768]{1,0:T(8,128)(2,1)S(1)}, u32[]{:S(2)}, u32[]{:S(2)}) collective-permute-start(bf16[512,768]{1,0:T(8,128)(2,1)S(1)} %collective-permute-done.3.refs_5_.refs_7_.refs_11_), channel_id=1, source_target_pairs={{0,16},{16,32},{32,48},{48,64},{64,80},{80,96},{96,112},{112,0},{1... | collective-permute-start | bytes 2359304 | tf_op jit(solution)/shard_map/ppermute | solution.py:371
  64.7 19.4 %collective-permute-start.6 = (bf16[512,768]{1,0:T(8,128)(2,1)}, bf16[512,768]{1,0:T(8,128)(2,1)}, u32[]{:S(2)}, u32[]{:S(2)}) collective-permute-start(bf16[512,768]{1,0:T(8,128)(2,1)} %collective-permute-done.4.refs_6_.refs_8_.refs_12_), channel_id=1, source_target_pairs={{0,112},{16,0},{32,16},{48,32},{64,48},{80,64},{96,80},{112,96},{1... | collective-permute-start | bytes 2359304 | tf_op jit(solution)/shard_map/ppermute | solution.py:371
  84.1 0.9 copy-start.17
  85.0 3.2 collective-permute-start.9
  85.0 21.4 %collective-permute-start.7 = (bf16[512,768]{1,0:T(8,128)(2,1)}, bf16[512,768]{1,0:T(8,128)(2,1)S(1)}, u32[]{:S(2)}, u32[]{:S(2)}) collective-permute-start(bf16[512,768]{1,0:T(8,128)(2,1)} %copy-done.17), channel_id=1, source_target_pairs={{0,16},{16,32},{32,48},{48,64},{64,80},{80,96},{96,112},{112,0},{1... | collective-permute-start | bytes 2359304 | tf_op jit(solution)/shard_map/ppermute | solution.py:371
  85.6 20.8 %collective-permute-start.8 = (bf16[512,768]{1,0:T(8,128)(2,1)}, bf16[512,768]{1,0:T(8,128)(2,1)}, u32[]{:S(2)}, u32[]{:S(2)}) collective-permute-start(bf16[512,768]{1,0:T(8,128)(2,1)} %collective-permute-done.6.refs_6_.refs_8_.refs_14_), channel_id=1, source_target_pairs={{0,112},{16,0},{32,16},{48,32},{64,48},{80,64},{96,80},{112,96},{1... | collective-permute-start | bytes 2359304 | tf_op jit(solution)/shard_map/ppermute | solution.py:371
  88.4 12.6 %copy-start.11 = (bf16[32,3072]{1,0:T(8,128)(2,1)S(1)}, bf16[32,3072]{1,0:T(8,128)(2,1)}, u32[]{:S(2)}) copy-start(bf16[32,3072]{1,0:T(8,128)(2,1)} %param.16) | copy-start | bytes 589828
  88.4 12.6 %collective-permute-start.10 = (f32[32,3072]{1,0:T(8,128)S(1)}, f32[32,3072]{1,0:T(8,128)S(1)}, u32[]{:S(2)}, u32[]{:S(2)}) collective-permute-start(f32[32,3072]{1,0:T(8,128)S(1)} %select_bitcast_fusion.2), channel_id=1, source_target_pairs={{0,128},{128,0},{1,129},{129,1},{2,130},{130,2},{3,131},{131,3},{4... | collective-permute-start | bytes 1179656 | tf_op jit(solution)/shard_map/ppermute | solution.py:387
  101.0 0.7 copy-start.13
  106.4 4.7 %copy-start.12 = (bf16[512,768]{1,0:T(8,128)(2,1)}, bf16[512,768]{1,0:T(8,128)(2,1)S(1)}, u32[]{:S(2)}) copy-start(bf16[512,768]{1,0:T(8,128)(2,1)S(1)} %collective-permute-done.7.refs_5_.refs_7_.refs_15_) | copy-start | bytes 2359300
  106.4 16.0 %collective-permute-start.13 = (bf16[32,768]{1,0:T(8,128)(2,1)S(1)}, bf16[32,768]{1,0:T(8,128)(2,1)S(1)}, u32[]{:S(2)}, u32[]{:S(2)}) collective-permute-start(bf16[32,768]{1,0:T(8,128)(2,1)S(1)} %convolution_convert_fusion), channel_id=1, source_target_pairs={{0,8},{8,0},{1,9},{9,1},{2,10},{10,2},{3,11},{11,3},{4,12},{12,4},... | collective-permute-start | bytes 147464 | tf_op jit(solution)/shard_map/ppermute | solution.py:396
  106.4 16.0 %collective-permute-start.11 = (bf16[256,768]{1,0:T(8,128)(2,1)S(1)}, bf16[256,768]{1,0:T(8,128)(2,1)S(1)}, u32[]{:S(2)}, u32[]{:S(2)}) collective-permute-start(bf16[256,768]{1,0:T(8,128)(2,1)S(1)} %slice.78), channel_id=1, source_target_pairs={{0,16},{16,32},{32,48},{48,64},{64,80},{80,96},{96,112},{112,0},{1... | collective-permute-start | bytes 1179656 | tf_op jit(solution)/shard_map/ppermute | solution.py:374
  108.5 14.0 %copy-start.1 = (bf16[512,384]{1,0:T(8,128)(2,1)S(1)}, bf16[512,384]{1,0:T(8,128)(2,1)}, u32[]{:S(2)}) copy-start(bf16[512,384]{1,0:T(8,128)(2,1)} %copy-done) | copy-start | bytes 1179652
  108.5 14.0 %copy-start.3 = (bf16[512,384]{1,0:T(8,128)(2,1)S(1)}, bf16[512,384]{1,0:T(8,128)(2,1)}, u32[]{:S(2)}) copy-start(bf16[512,384]{1,0:T(8,128)(2,1)} %copy-done.2) | copy-start | bytes 1179652
  108.5 14.0 %copy-start.5 = (bf16[512,384]{1,0:T(8,128)(2,1)S(1)}, bf16[512,384]{1,0:T(8,128)(2,1)}, u32[]{:S(2)}) copy-start(bf16[512,384]{1,0:T(8,128)(2,1)} %copy-done.4) | copy-start | bytes 1179652
  108.5 14.0 %copy-start.7 = (bf16[512,384]{1,0:T(8,128)(2,1)S(1)}, bf16[512,384]{1,0:T(8,128)(2,1)}, u32[]{:S(2)}) copy-start(bf16[512,384]{1,0:T(8,128)(2,1)} %copy-done.6) | copy-start | bytes 1179652
  108.5 13.9 %collective-permute-start.12 = (bf16[256,768]{1,0:T(8,128)(2,1)S(1)}, bf16[256,768]{1,0:T(8,128)(2,1)S(1)}, u32[]{:S(2)}, u32[]{:S(2)}) collective-permute-start(bf16[256,768]{1,0:T(8,128)(2,1)S(1)} %slice.79), channel_id=1, source_target_pairs={{0,112},{16,0},{32,16},{48,32},{64,48},{80,64},{96,80},{112,96},{1... | collective-permute-start | bytes 1179656 | tf_op jit(solution)/shard_map/ppermute | solution.py:374
  323.2 6.6 %collective-permute-start.14 = (bf16[1024,384]{1,0:T(8,128)(2,1)S(1)}, bf16[1024,384]{1,0:T(8,128)(2,1)S(1)}, u32[]{:S(2)}, u32[]{:S(2)}) collective-permute-start(bf16[1024,384]{1,0:T(8,128)(2,1)S(1)} %get-tuple-element.63), channel_id=1, source_target_pairs={{0,8},{8,0},{1,9},{9,1},{2,10},{10,2},{3,11},{11,3},{4,12},{12,4},... | collective-permute-start | bytes 2359304 | tf_op jit(solution)/shard_map/ppermute | solution.py:405
  323.3 5.6 %collective-permute-start.18 = (bf16[2,32,768]{2,1,0:T(8,128)(2,1)S(1)}, bf16[2,32,768]{2,1,0:T(8,128)(2,1)S(1)}, u32[]{:S(2)}, u32[]{:S(2)}) collective-permute-start(bf16[2,32,768]{2,1,0:T(8,128)(2,1)S(1)} %maximum_select_fusion.1), channel_id=1, source_target_pairs={{0,128},{128,0},{1,129},{129,1},{2,130},{130,2},{3,131},{131,3},{4... | collective-permute-start | bytes 294920 | tf_op jit(solution)/shard_map/ppermute | solution.py:399
  324.5 5.3 %collective-permute-start.15 = (f32[3,2,1024]{2,1,0:T(2,128)S(1)}, f32[3,2,1024]{2,1,0:T(2,128)S(1)}, u32[]{:S(2)}, u32[]{:S(2)}) collective-permute-start(f32[3,2,1024]{2,1,0:T(2,128)S(1)} %get-tuple-element.64), channel_id=1, source_target_pairs={{0,8},{8,0},{1,9},{9,1},{2,10},{10,2},{3,11},{11,3},{4,12},{12,4},... | collective-permute-start | bytes 73736 | tf_op jit(solution)/shard_map/ppermute | solution.py:406
  324.6 5.2 %collective-permute-start.17 = (f32[3,2,1024]{2,1,0:T(2,128)S(1)}, f32[3,2,1024]{2,1,0:T(2,128)S(1)}, u32[]{:S(2)}, u32[]{:S(2)}) collective-permute-start(f32[3,2,1024]{2,1,0:T(2,128)S(1)} %get-tuple-element.64), channel_id=1, source_target_pairs={{0,136},{8,128},{128,8},{136,0},{1,137},{9,129},{129,9},{137,1},{2... | collective-permute-start | bytes 73736 | tf_op jit(solution)/shard_map/ppermute | solution.py:408
  325.5 4.3 %collective-permute-start.16 = (f32[3,2,1024]{2,1,0:T(2,128)S(1)}, f32[3,2,1024]{2,1,0:T(2,128)S(1)}, u32[]{:S(2)}, u32[]{:S(2)}) collective-permute-start(f32[3,2,1024]{2,1,0:T(2,128)S(1)} %get-tuple-element.65.lr_own), channel_id=1, source_target_pairs={{0,128},{128,0},{1,129},{129,1},{2,130},{130,2},{3,131},{131,3},{4... | collective-permute-start | bytes 73736 | tf_op jit(solution)/shard_map/ppermute | solution.py:407
  329.9 22.2 %collective-permute-start.20 = (bf16[4,384,1536]{2,1,0:T(8,128)(2,1)}, bf16[4,384,1536]{2,1,0:T(8,128)(2,1)S(1)}, u32[]{:S(2)}, u32[]{:S(2)}) collective-permute-start(bf16[4,384,1536]{2,1,0:T(8,128)(2,1)} %bitcast.61), channel_id=1, source_target_pairs={{0,8},{8,0},{1,9},{9,1},{2,10},{10,2},{3,11},{11,3},{4,12},{12,4},... | collective-permute-start | bytes 14155784 | tf_op jit(solution)/shard_map/ppermute | solution.py:412
  330.0 19.1 %copy-start.8 = (bf16[1536,1536]{1,0:T(8,128)(2,1)S(1)}, bf16[1536,1536]{1,0:T(8,128)(2,1)}, u32[]{:S(2)}) copy-start(bf16[1536,1536]{1,0:T(8,128)(2,1)} %all-gather.5.cloned.1.call-done) | copy-start | bytes 14155780
  351.0 8.9 %collective-permute-start.19 = (bf16[64,1536]{1,0:T(8,128)(2,1)S(1)}, bf16[64,1536]{1,0:T(8,128)(2,1)S(1)}, u32[]{:S(2)}, u32[]{:S(2)}) collective-permute-start(bf16[64,1536]{1,0:T(8,128)(2,1)S(1)} %get-tuple-element.78), channel_id=1, source_target_pairs={{0,1},{1,0},{2,3},{3,2},{4,5},{5,4},{6,7},{7,6},{8,9},{9,8},{10,11... | collective-permute-start | bytes 589832 | tf_op jit(solution)/shard_map/ppermute | solution.py:422
  354.0 8.5 %collective-permute-start.21 = (bf16[64,1536]{1,0:T(8,128)(2,1)S(1)}, bf16[64,1536]{1,0:T(8,128)(2,1)S(1)}, u32[]{:S(2)}, u32[]{:S(2)}) collective-permute-start(bf16[64,1536]{1,0:T(8,128)(2,1)S(1)} %get-tuple-element.80), channel_id=1, source_target_pairs={{0,1},{1,0},{2,3},{3,2},{4,5},{5,4},{6,7},{7,6},{8,9},{9,8},{10,11... | collective-permute-start | bytes 589832 | tf_op jit(solution)/shard_map/ppermute | solution.py:422
Sparse Core Ops, SparseCore 0:
  9.1 45.7 all-gather.6
  56.8 53.7 all-gather.4
